TPU v7x, 32 devices: a whole 2x2x4 slice. The times are simulated.
32 devices in a mesh: row: 4 (over y, core), col: 8 (over z, x).
Axes of the slice: x: 2, y: 2, z: 4, core: 2. Of those that a mesh axis runs over, the one named last changes fastest.
Arguments:
- hidden_states: bfloat16 [512, 2048], P('col', 'row'), may hold values from -20 to 20
- input_gain: float32 [2, 2048], P(None, 'row'), may hold values from 0.25 to 1.75
- inner_weight: bfloat16 [2, 2048, 2, 4096], P(None, 'row', None, 'col'), may hold values from -0.125 to 0.125
- proj_weight: bfloat16 [2, 2048, 256], P(None, 'row'), may hold values from -0.125 to 0.125
- step_weight: bfloat16 [2, 2048, 64], P(None, 'row', 'col'), may hold values from -0.125 to 0.125
- inner_kernel: float32 [2, 4, 4096], P(None, None, 'col'), may hold values from -3 to 3
- proj_kernel: float32 [2, 4, 256], replicated, may hold values from -3 to 3
- step_bias: float32 [2, 64], P(None, 'col'), may hold values from -5 to -1
- decay_log: float32 [2, 64], P(None, 'col'), may hold values from -2 to 1
- skip_gain: float32 [2, 64], P(None, 'col'), may hold values from 0.5 to 1.5
- norm_gain: float32 [2, 4096], P(None, 'col'), may hold values from 0.25 to 1.75
- out_weight: bfloat16 [2, 4096, 2048], P(None, 'col', 'row'), may hold values from -0.09375 to 0.09375
- inner_cache: bfloat16 [2, 32, 3, 4096], P(None, 'row', None, 'col'), may hold values from -6 to 6
- proj_cache: bfloat16 [2, 32, 3, 256], P(None, 'row'), may hold values from -6 to 6
- state_cache: float32 [2, 32, 64, 64, 128], P(None, 'row', 'col'), may hold values from -1.2 to 1.2
- accepted: int32 [32], P('row'), may hold values from 1 to 16
- owners: int32 [32], P('row'), may hold values from 0 to 7, as said below
- tenant_ranges: int32 [4, 2], replicated, may hold values from 0 to 32, as said below
Outputs:
- hidden_output: bfloat16 [512, 2048], P('col', 'row')
- step_states: bfloat16 [2, 32, 16, 64, 64, 128], P(None, 'row', None, 'col')
- owned_states: bfloat16 [4, 8, 2, 2, 64, 64, 128], P('row', 'col')
Inputs may be any that keep to these rules, and one draw needn't show every extreme that they name: `owners`: within the requests of one index of row (aligned blocks of 8) no owner appears more than 2 times, and in every block some owner appears exactly 2 times. `tenant_ranges`: the ranges are in order, disjoint and not empty; exactly 4 requests lie in no range.
All inputs are finite; a program needn't handle non-finite values.
Results may differ from a plain program's by a relative error of at most 0.024.
Values may be sent and summed in bfloat16 or wider, within the bound.
A program may use at most 192 MiB of HBM per device.

v0:
```python
import jax
import jax.numpy as jnp
from jax import lax
from jax.sharding import PartitionSpec as P

S = 16
SEND_CAP = 2


EPSILON = 1e-05


def conv_silu(prefix, incoming, kernel):
    joined = jnp.concatenate([prefix, incoming], axis=1)
    length = incoming.shape[1]
    summed = joined[:, 0:length, :] * kernel[0]
    for offset in range(1, kernel.shape[0]):
        summed = summed + joined[:, offset : offset + length, :] * kernel[offset]
    return jax.nn.silu(summed)


def ssm_scan(decays, deltas, inner_values, b_values, c_values, skip_values, start_state):

    def advance(carried, packed):
        decay_now, delta_now, value_now, b_now, c_now = packed
        updated = (
            decay_now[:, :, None, None] * carried
            + (delta_now[:, :, None] * value_now)[:, :, :, None] * b_now[:, None, None, :]
        )
        output = (
            jnp.einsum("rhpn,rn->rhp", updated, c_now, precision=lax.Precision.HIGHEST)
            + skip_values[None, :, None] * value_now
        )
        return (updated, (output, updated.astype(jnp.bfloat16)))

    time_major = tuple(
        (
            jnp.moveaxis(member, 1, 0)
            for member in (decays, deltas, inner_values, b_values, c_values)
        )
    )
    last_state, (outputs, states) = lax.scan(advance, start_state, time_major)
    return (jnp.moveaxis(outputs, 0, 1), jnp.moveaxis(states, 0, 1))


def local(
    hidden_states,
    input_gain,
    inner_weight,
    proj_weight,
    step_weight,
    inner_kernel,
    proj_kernel,
    step_bias,
    decay_log,
    skip_gain,
    norm_gain,
    out_weight,
    inner_cache,
    proj_cache,
    state_cache,
    accepted,
    owners,
    tenant_ranges,
):
    layer_count = inner_weight.shape[0]
    row_width = inner_weight.shape[1]
    inner_local = inner_weight.shape[3]
    heads_local = step_weight.shape[2]
    head_size = inner_local // heads_local
    state_size = proj_weight.shape[2] // 2
    requests_local = state_cache.shape[1]
    draft_steps = S
    row_count = lax.axis_size("row")
    col_count = lax.axis_size("col")
    model_width = row_width * row_count
    inner_width = inner_local * col_count
    token_rows = requests_local * draft_steps
    local_ids = jnp.arange(requests_local, dtype=jnp.int32)
    request_ids = lax.axis_index("row") * requests_local + local_ids
    live_mask = jnp.any(
        (request_ids[:, None] >= tenant_ranges[None, :, 0])
        & (request_ids[:, None] < tenant_ranges[None, :, 1]),
        axis=1,
    )
    earlier = (owners[:, None] == owners[None, :]) & (local_ids[None, :] < local_ids[:, None])
    slot_ranks = jnp.sum(earlier.astype(jnp.int32), axis=1)
    slot_ids = owners * SEND_CAP + slot_ranks
    slot_grid = jnp.arange(col_count * SEND_CAP, dtype=jnp.int32)
    step_grid = jnp.arange(draft_steps, dtype=jnp.int32)
    picker = (
        (slot_grid[:, None, None] == slot_ids[None, :, None])
        & (step_grid[None, None, :] == accepted[None, :, None] - 1)
        & live_mask[None, :, None]
    )
    picker = picker.astype(jnp.bfloat16).reshape(col_count * SEND_CAP, token_rows)
    hidden = hidden_states
    step_outputs = []
    chosen_layers = []
    for layer_index in range(layer_count):
        all_tokens = lax.all_gather(hidden, "col", axis=0, tiled=True)
        tokens_f = all_tokens.astype(jnp.float32)
        scaled = (tokens_f * input_gain[layer_index]).astype(jnp.bfloat16)
        square_part = jnp.sum(tokens_f * tokens_f, axis=1)
        inner_part = jnp.dot(
            scaled,
            inner_weight[layer_index].reshape(row_width, 2 * inner_local),
            preferred_element_type=jnp.float32,
        )
        step_part = jnp.dot(scaled, step_weight[layer_index], preferred_element_type=jnp.float32)
        proj_part = jnp.dot(scaled, proj_weight[layer_index], preferred_element_type=jnp.float32)
        inner_sum, step_sum, proj_sum, square_sum = (
            lax.psum_scatter(inner_part, "row", scatter_dimension=0, tiled=True),
            lax.psum_scatter(step_part, "row", scatter_dimension=0, tiled=True),
            lax.psum_scatter(proj_part, "row", scatter_dimension=0, tiled=True),
            lax.psum_scatter(square_part, "row", scatter_dimension=0, tiled=True),
        )
        inverse_rms = lax.rsqrt(square_sum / model_width + EPSILON)
        inner_vals = inner_sum * inverse_rms[:, None]
        gate_vals = inner_vals[:, :inner_local]
        raw_inner = inner_vals[:, inner_local:].reshape(requests_local, draft_steps, inner_local)
        raw_proj = (proj_sum * inverse_rms[:, None]).reshape(
            requests_local, draft_steps, 2 * state_size
        )
        conv_inner = conv_silu(
            inner_cache[layer_index].astype(jnp.float32), raw_inner, inner_kernel[layer_index]
        )
        conv_proj = conv_silu(
            proj_cache[layer_index].astype(jnp.float32), raw_proj, proj_kernel[layer_index]
        )
        deltas = jax.nn.softplus(
            (step_sum * inverse_rms[:, None]).reshape(requests_local, draft_steps, heads_local)
            + step_bias[layer_index]
        )
        decays = jnp.exp(-deltas * jnp.exp(decay_log[layer_index]))
        outputs, states = ssm_scan(
            decays,
            deltas,
            conv_inner.reshape(requests_local, draft_steps, heads_local, head_size),
            conv_proj[..., :state_size],
            conv_proj[..., state_size:],
            skip_gain[layer_index],
            state_cache[layer_index],
        )
        step_outputs.append(states)
        gated_raw = outputs.reshape(token_rows, inner_local) * jax.nn.silu(gate_vals)
        gate_square = lax.psum(jnp.sum(gated_raw * gated_raw, axis=1), "col")
        gated = (
            gated_raw
            * norm_gain[layer_index]
            * lax.rsqrt(gate_square / inner_width + EPSILON)[:, None]
        ).astype(jnp.bfloat16)
        layer_weight = out_weight[layer_index]
        partial_out = jnp.dot(
            lax.all_gather(gated, "row", axis=0, tiled=True),
            layer_weight,
            preferred_element_type=jnp.float32,
        )
        out_sum = lax.psum_scatter(
            partial_out.astype(jnp.bfloat16), "col", scatter_dimension=0, tiled=True
        ).astype(jnp.float32)
        hidden = (hidden.astype(jnp.float32) + out_sum).astype(jnp.bfloat16)
        chosen = jnp.dot(
            picker,
            states.reshape(token_rows, heads_local * head_size * state_size),
            preferred_element_type=jnp.float32,
        )
        chosen = chosen.astype(jnp.bfloat16).reshape(
            col_count, SEND_CAP, heads_local, head_size, state_size
        )
        chosen_layers.append(chosen)
    gathered = lax.all_to_all(
        jnp.stack(chosen_layers, axis=2), "col", split_axis=0, concat_axis=3, tiled=True
    )
    owned_block = gathered[None]
    step_all = jnp.stack(step_outputs, axis=0)
    return (hidden, step_all, owned_block)


def solution(mesh):
    placed = (
        P("col", "row"),
        P(None, "row"),
        P(None, "row", None, "col"),
        P(None, "row", None),
        P(None, "row", "col"),
        P(None, None, "col"),
        P(),
        P(None, "col"),
        P(None, "col"),
        P(None, "col"),
        P(None, "col"),
        P(None, "col", "row"),
        P(None, "row", None, "col"),
        P(None, "row", None, None),
        P(None, "row", "col", None, None),
        P("row"),
        P("row"),
        P(),
    )
    return jax.shard_map(
        local,
        mesh=mesh,
        in_specs=placed,
        out_specs=(
            P("col", "row"),
            P(None, "row", None, "col", None, None),
            P("row", "col", None, None, None, None, None),
        ),
        check_vma=False,
    )
```

profile of v0, /device:TPU:0, one launch (start us, length us, event | category | flops | bytes accessed | tf_op | source)
XLA Modules:
  0.0 858.5 jit_solution(3359093773446312716)
XLA Ops:
  8.0 33.2 %all_gather.12 = bf16[512,512]{1,0:T(8,128)(2,1)S(1)} all-gather(bf16[64,512]{1,0:T(8,128)(2,1)} %param.22), channel_id=1, replica_groups=mesh['row'=4,'col'=8] {'col'}, dimensions={0}, use_global_device_ids=true | all-gather | bytes 589824 | tf_op jit(solution)/shard_map/all_gather | solution.py:101
  45.0 3.5 fusion.71
  52.8 5.7 all-reduce
  60.3 4.1 slice_bitcast_fusion.1
  65.4 22.4 %reduce-scatter.13.cloned.1.call-done = f32[128,256]{1,0:T(8,128)} async-done(((f32[512,256]{1,0:T(8,128)}), f32[128,256]{1,0:T(8,128)}) %reduce-scatter.13.cloned.1.call-update) | async-done | bytes 131088 | tf_op jit(solution)/shard_map/reduce_scatter | solution.py:115
  88.9 33.4 %reduce-scatter.11.cloned.1.call-done = f32[128,1024]{1,0:T(8,128)} async-done(((f32[512,1024]{1,0:T(8,128)}), f32[128,1024]{1,0:T(8,128)}) %reduce-scatter.11.cloned.1.call-update) | async-done | bytes 524304 | tf_op jit(solution)/shard_map/reduce_scatter | solution.py:113
  124.8 6.4 broadcast.154.clone2
  131.2 160.2 %while.28 = (s32[]{:T(128)}, f32[8,8,64,128]{3,2,1,0:T(8,128)}, f32[16,8,8,64]{3,2,1,0:T(8,128)S(1)}, bf16[16,8,8,64,128]{4,3,2,0,1:T(8,128)(2,1)}, f32[16,8,8]{...) while((s32[]{:T(128)}, f32[8,8,64,128]{3,2,1,0:T(8,128)}, ...), condition=%wide.region_6.0_spmd, body=%wide.region_5.0_spmd.sunk | while | flops 8400898 | bytes 7530637 | solution.py:42
  134.6 6.5 fusion.99
  144.6 6.5 fusion.99
  151.3 3.3 bitcast_dynamic-update-slice_fusion.8
  154.6 6.5 fusion.99
  164.6 6.5 fusion.99
  171.3 3.3 bitcast_dynamic-update-slice_fusion.8
  174.6 6.5 fusion.99
  184.6 6.5 fusion.99
  194.6 6.5 fusion.99
  204.6 6.5 fusion.99
  211.4 3.3 bitcast_dynamic-update-slice_fusion.8
  214.7 6.5 fusion.99
  224.7 6.5 fusion.99
  231.4 3.3 bitcast_dynamic-update-slice_fusion.8
  234.7 6.5 fusion.99
  244.7 6.5 fusion.99
  254.7 6.5 fusion.99
  264.7 6.5 fusion.99
  271.4 3.3 bitcast_dynamic-update-slice_fusion.8
  274.8 6.5 fusion.99
  281.5 3.3 bitcast_dynamic-update-slice_fusion.8
  284.8 6.5 fusion.99
  292.8 21.4 %psum.14 = f32[128]{0:T(128)S(1)} all-reduce(f32[128]{0:T(128)S(1)} %get-tuple-element.159), channel_id=1, replica_groups=mesh['row'=4,'col'=8] {'col'}, use_global_device_ids=true, to_apply=%region_8.9 | all-reduce | flops 128 | bytes 1024 | tf_op jit(solution)/shard_map/psum | solution.py:147
  314.3 6.6 all_gather.13
  323.3 59.0 %reduce-scatter.15.cloned.1.call-done = bf16[64,512]{1,0:T(8,128)(2,1)} async-done(((bf16[512,512]{1,0:T(8,128)(2,1)}), bf16[64,512]{1,0:T(8,128)(2,1)}) %reduce-scatter.15.cloned.1.call-update) | async-done | bytes 65552 | tf_op jit(solution)/shard_map/reduce_scatter | solution.py:159
  383.1 31.5 %all_gather.14 = bf16[512,512]{1,0:T(8,128)(2,1)S(1)} all-gather(bf16[64,512]{1,0:T(8,128)(2,1)S(1)} %add_convert_fusion.1), channel_id=1, replica_groups=mesh['row'=4,'col'=8] {'col'}, dimensions={0}, use_global_device_ids=true | all-gather | bytes 589824 | tf_op jit(solution)/shard_map/all_gather | solution.py:101
  421.1 20.1 %reshape.291 = bf16[128,65536]{1,0:T(8,128)(2,1)} reshape(bf16[8,16,8,64,128]{4,3,2,1,0:T(8,128)(2,1)} %bitcast.250) | data formatting | bytes 33554432 | tf_op jit(solution)/shard_map/reshape | solution.py:165
  441.2 8.3 fusion.2
  451.4 6.1 all-reduce.1
  459.7 32.9 %reduce-scatter.19.cloned.1.call-done = f32[128,1024]{1,0:T(8,128)} async-done(((f32[512,1024]{1,0:T(8,128)}), f32[128,1024]{1,0:T(8,128)}) %reduce-scatter.19.cloned.1.call-update) | async-done | bytes 524304 | tf_op jit(solution)/shard_map/reduce_scatter | solution.py:113
  495.2 6.4 broadcast.154.clone
  501.5 135.0 %while.29 = (s32[]{:T(128)}, f32[8,8,64,128]{3,2,1,0:T(8,128)S(1)}, f32[16,8,8,64]{3,2,1,0:T(8,128)S(1)}, bf16[16,8,8,64,128]{4,3,2,0,1:T(8,128)(2,1)}, f32[16,8...) while((s32[]{:T(128)}, f32[8,8,64,128]{3,2,1,0:T(8,128)S(1)}, ...), condition=%wide.region_16.17_spmd, body=%wide.region_15.16_spmd.sunk | while | flops 8400898 | bytes 7514253 | solution.py:42
  504.1 5.0 fusion.102
  512.6 5.0 fusion.102
  521.0 5.0 fusion.102
  529.4 5.0 fusion.102
  537.9 5.0 fusion.102
  546.3 5.0 fusion.102
  554.8 5.0 fusion.102
  563.2 5.0 fusion.102
  571.6 5.0 fusion.102
  580.1 5.0 fusion.102
  588.5 5.0 fusion.102
  596.9 5.0 fusion.102
  605.4 5.0 fusion.102
  613.8 5.0 fusion.102
  622.3 5.0 fusion.102
  630.7 5.0 fusion.102
  636.5 20.1 %reshape.292 = bf16[128,65536]{1,0:T(8,128)(2,1)} reshape(bf16[8,16,8,64,128]{4,3,2,1,0:T(8,128)(2,1)} %bitcast.248) | data formatting | bytes 33554432 | tf_op jit(solution)/shard_map/reshape | solution.py:165
  656.6 8.0 fusion.3
  668.6 5.5 all-to-all-start
  674.6 84.8 %psum.15 = f32[128]{0:T(128)S(1)} all-reduce(f32[128]{0:T(128)S(1)} %get-tuple-element.157), channel_id=1, replica_groups=mesh['row'=4,'col'=8] {'col'}, use_global_device_ids=true, to_apply=%region_18.19 | all-reduce | flops 128 | bytes 1024 | tf_op jit(solution)/shard_map/psum | solution.py:147
  759.5 6.5 all_gather.15
  767.2 23.0 %pad_maximum_fusion = bf16[2,8,16,8,64,128]{5,4,3,2,1,0:T(8,128)(2,1)} fusion(bf16[1,8,16,8,64,128]{5,4,3,2,1,0:T(8,128)(2,1)} %bitcast.249, bf16[1,8,16,8,64,128]{5,4,3,2,1,0:T(8,128)(2,1)} %bitcast.251), kind=kLoop, calls=%fused_computation.22 | loop fusion | flops 16777216 | bytes 67108864 | tf_op jit(solution)/shard_map/stack | solution.py:176
  790.2 54.2 %reduce-scatter.23.cloned.1.call-done = bf16[64,512]{1,0:T(8,128)(2,1)} async-done(((bf16[512,512]{1,0:T(8,128)(2,1)}), bf16[64,512]{1,0:T(8,128)(2,1)}) %reduce-scatter.23.cloned.1.call-update) | async-done | bytes 65552 | tf_op jit(solution)/shard_map/reduce_scatter | solution.py:159
  845.9 5.8 copy.85
  (330 shorter events, 130.3 us)
Async XLA Ops:
  7.2 57.3 %reduce-scatter.9.cloned.1.call-start = ((), (), s32[]{:S(2)}) async-start(), calls=%async_computation.9 | async-start | bytes 20480 | tf_op jit(solution)/shard_map/reduce_scatter | solution.py:114
  42.8 44.9 %reduce-scatter.13.cloned.1.call-start = ((), (), s32[]{:S(2)}) async-start(), calls=%async_computation.11 | async-start | bytes 655360 | tf_op jit(solution)/shard_map/reduce_scatter | solution.py:115
  44.9 77.4 %reduce-scatter.11.cloned.1.call-start = ((), (), s32[]{:S(2)}) async-start(), calls=%async_computation.10 | async-start | bytes 2621440 | tf_op jit(solution)/shard_map/reduce_scatter | solution.py:113
  48.7 2.2 copy-start.4
  50.7 0.7 copy-start.22
  50.7 7.8 copy-start.14
  50.7 7.8 copy-start.16
  50.7 7.8 copy-start.17
  50.7 8.4 copy-start.11
  50.8 8.9 %copy-start.10 = (f32[2,4,256]{2,1,0:T(4,128)S(1)}, f32[2,4,256]{2,1,0:T(4,128)}, u32[]{:S(2)}) copy-start(f32[2,4,256]{2,1,0:T(4,128)} %param.28) | copy-start | bytes 24580
  50.8 8.9 %copy-start.6 = (f32[2,4,512]{2,1,0:T(4,128)S(1)}, f32[2,4,512]{2,1,0:T(4,128)}, u32[]{:S(2)}) copy-start(f32[2,4,512]{2,1,0:T(4,128)} %param.27) | copy-start | bytes 49156
  50.8 9.5 %copy-start.5 = (bf16[2,8,3,256]{3,1,2,0:T(8,128)(2,1)S(1)}, bf16[2,8,3,256]{3,1,2,0:T(8,128)(2,1)}, u32[]{:S(2)}) copy-start(bf16[2,8,3,256]{3,1,2,0:T(8,128)(2,1)} %param.35) | copy-start | bytes 73732
  50.8 331.4 %reduce-scatter.15.cloned.1.call-start = ((), (), s32[]{:S(2)}) async-start(), calls=%async_computation.12 | async-start | bytes 589824 | tf_op jit(solution)/shard_map/reduce_scatter | solution.py:159
  123.4 0.8 copy-start.1
  291.6 90.6 %copy-start.3 = (bf16[64,512]{1,0:T(8,128)(2,1)S(1)}, bf16[64,512]{1,0:T(8,128)(2,1)}, u32[]{:S(2)}) copy-start(bf16[64,512]{1,0:T(8,128)(2,1)} %param.22) | copy-start | bytes 196612
  292.8 121.8 %copy-start.19 = (bf16[2,512,8]{1,2,0:T(8,128)(2,1)S(1)}, bf16[2,512,8]{1,2,0:T(8,128)(2,1)}, u32[]{:S(2)}) copy-start(bf16[2,512,8]{1,2,0:T(8,128)(2,1)} %param.26) | copy-start | bytes 49156
  314.3 101.2 %copy-start.2 = (bf16[2,512,256]{2,1,0:T(8,128)(2,1)S(1)}, bf16[2,512,256]{2,1,0:T(8,128)(2,1)}, u32[]{:S(2)}) copy-start(bf16[2,512,256]{2,1,0:T(8,128)(2,1)} %param.25) | copy-start | bytes 1572868
  323.2 134.3 %reduce-scatter.17.cloned.1.call-start = ((), (), s32[]{:S(2)}) async-start(), calls=%async_computation.13 | async-start | bytes 20480 | tf_op jit(solution)/shard_map/reduce_scatter | solution.py:114
  415.5 43.1 %reduce-scatter.21.cloned.1.call-start = ((), (), s32[]{:S(2)}) async-start(), calls=%async_computation.15 | async-start | bytes 655360 | tf_op jit(solution)/shard_map/reduce_scatter | solution.py:115
  416.7 75.9 %reduce-scatter.19.cloned.1.call-start = ((), (), s32[]{:S(2)}) async-start(), calls=%async_computation.14 | async-start | bytes 2621440 | tf_op jit(solution)/shard_map/reduce_scatter | solution.py:113
  418.4 2.1 copy-start.21
  418.4 2.3 copy-start.15
  418.4 2.4 copy-start.20
  449.5 8.9 %copy-start.12 = (f32[8]{0:T(128)S(1)}, f32[8]{0:T(128)}, u32[]{:S(2)}) copy-start(f32[8]{0:T(128)} %get-tuple-element.205) | copy-start | bytes 100
  449.5 8.9 %copy-start.13 = (f32[8]{0:T(128)S(1)}, f32[8]{0:T(128)}, u32[]{:S(2)}) copy-start(f32[8]{0:T(128)} %get-tuple-element.209) | copy-start | bytes 100
  451.4 42.4 %copy-start.7 = (f32[1,1,512]{2,1,0:T(1,128)S(1)}, f32[1,1,512]{2,1,0:T(1,128)}, u32[]{:S(2)}) copy-start(f32[1,1,512]{2,1,0:T(1,128)} %get-tuple-element.187) | copy-start | bytes 6148
  451.4 42.4 %copy-start.8 = (f32[1,1,512]{2,1,0:T(1,128)S(1)}, f32[1,1,512]{2,1,0:T(1,128)}, u32[]{:S(2)}) copy-start(f32[1,1,512]{2,1,0:T(1,128)} %get-tuple-element.188) | copy-start | bytes 6148
  664.7 1.6 copy-start
  668.6 177.2 %all-to-all-start = ((bf16[8,2,2,8,64,128]{5,4,3,1,2,0:T(8,128)(2,1)}), bf16[8,2,2,8,64,128]{5,4,3,1,2,0:T(8,128)(2,1)}, u32[]{:S(2)}, u32[]{:S(2)}) async-start(bf16[8,2,2,8,64,128]{5,4,3,1,2,0:T(8,128)(2,1)} %pad_maximum_fusion.1), calls=%async_computation.8 | async-start | bytes 8388608 | tf_op jit(solution)/shard_map/all_to_all | solution.py:172
  674.1 85.2 %copy-start.9 = (f32[1,512]{1,0:T(1,128)S(1)}, f32[1,512]{1,0:T(1,128)}, u32[]{:S(2)}) copy-start(f32[1,512]{1,0:T(1,128)} %get-tuple-element.197) | copy-start | bytes 6148
  674.2 91.8 %copy-start.18 = (bf16[2,512,512]{2,1,0:T(8,128)(2,1)S(1)}, bf16[2,512,512]{2,1,0:T(8,128)(2,1)}, u32[]{:S(2)}) copy-start(bf16[2,512,512]{2,1,0:T(8,128)(2,1)} %param.33) | copy-start | bytes 3145732
  674.2 170.2 %reduce-scatter.23.cloned.1.call-start = ((), (), s32[]{:S(2)}) async-start(), calls=%async_computation.16 | async-start | bytes 589824 | tf_op jit(solution)/shard_map/reduce_scatter | solution.py:159
Sparse Core Ops, SparseCore 0:
  42.9 20.4 reduce-scatter.8
  66.0 21.6 reduce-scatter.12
  90.8 31.4 reduce-scatter.10
  323.4 58.8 reduce-scatter.14
  415.6 18.2 reduce-scatter.16
  436.3 21.7 reduce-scatter.20
  461.2 31.3 reduce-scatter.18
  767.3 76.9 reduce-scatter.22
where the time goes:
time: 863 us; the launch traced here: 858 us
  matrix products  213 us (25%)
  waiting for transfers between devices  202 us (23%)
  blocking collectives  196 us (23%)
  other arithmetic  147 us (17%)
  local copies, waits for them, and re-layouts  78.6 us (9%)
  between operations  15.4 us (2%)
    dot_general x32, matrix products, advance(): jnp.einsum('rhpn,rn->rhp', updated, c_now, precision=lax.Precision.HIGHEST)  184 us
    reduce_scatter x2, waiting for transfers between devices, local(): lax.psum_scatter(partial_out.astype(jnp.bfloat16), 'col', scatter_dimensi...  113 us
    psum x2, blocking collectives, local(): gate_square = lax.psum(jnp.sum(gated_raw * gated_raw, axis=1), 'col')  106 us
    dynamic_update_slice x64, other arithmetic, ssm_scan(): last_state, (outputs, states) = lax.scan(advance, start_state, time_major)  95.7 us
    reduce_scatter x2, waiting for transfers between devices, local(): lax.psum_scatter(inner_part, 'row', scatter_dimension=0, tiled=True)  66.3 us
    all_gather x2, blocking collectives, local(): all_tokens = lax.all_gather(hidden, 'col', axis=0, tiled=True)  64.7 us
    reshape x2, local copies, waits for them, and re-layouts, local(): states.reshape(token_rows, heads_local * head_size * state_size)  40.2 us
    another operation x1, other arithmetic, local(): step_all = jnp.stack(step_outputs, axis=0)  23 us
  transfers between devices with their start and end apart: 9, of which 5 were waited for; matrix products, arithmetic and copies ran while one was open for 9% of the time, Pallas kernels for 0%

commit v1 on v0

v1 whole, which is shorter than its diff:
```python
import functools

import jax
import jax.numpy as jnp
from jax import lax
from jax.experimental import pallas as pl
from jax.experimental.pallas import tpu as pltpu
from jax.sharding import PartitionSpec as P

S = 16
SEND_CAP = 2
EPSILON = 1e-05
LANES = 128
F32 = jnp.float32
BF16 = jnp.bfloat16
HIGH = lax.Precision.HIGHEST
VMEM_LIMIT = 48 * 1024 * 1024


def dot_nt(a, b, precision=None):
    return lax.dot_general(
        a, b, (((1,), (1,)), ((), ())), precision=precision, preferred_element_type=F32
    )


def dot_tn(a, b, precision=None):
    return lax.dot_general(
        a, b, (((0,), (0,)), ((), ())), precision=precision, preferred_element_type=F32
    )


def pick_kernel(count, slots, state_ref, *out_refs):
    for offset in range(count):
        for slot in range(SEND_CAP):
            request = slots[offset * SEND_CAP + slot]
            out_refs[offset][slot, 0] = state_ref[0, request].astype(BF16)


def pick_states(slot_requests, state_cache, count):
    layers, requests, heads, size, state = state_cache.shape
    out_block = pl.BlockSpec(
        (SEND_CAP, 1, heads, size, state), lambda layer, slots: (0, layer, 0, 0, 0)
    )
    return pl.pallas_call(
        functools.partial(pick_kernel, count),
        grid_spec=pltpu.PrefetchScalarGridSpec(
            num_scalar_prefetch=1,
            grid=(layers,),
            in_specs=[
                pl.BlockSpec(
                    (1, requests, heads, size, state), lambda layer, slots: (layer, 0, 0, 0, 0)
                )
            ],
            out_specs=[out_block] * count,
        ),
        out_shape=[jax.ShapeDtypeStruct((SEND_CAP, layers, heads, size, state), BF16)] * count,
        compiler_params=pltpu.CompilerParams(vmem_limit_bytes=VMEM_LIMIT),
        cost_estimate=pl.CostEstimate(
            flops=0, bytes_accessed=8 * 1024 * 1024, transcendentals=0
        ),
    )(slot_requests, state_cache)


def conv_silu(joined, prefix, incoming, kernel):
    taps = kernel.shape[0]
    length = incoming.shape[0]
    joined[8 - (taps - 1) : 8, :] = prefix
    joined[8 : 8 + length, :] = incoming
    first = 8 - (taps - 1)
    summed = joined[first : first + length, :] * kernel[0:1, :]
    for tap in range(1, taps):
        summed = summed + joined[first + tap : first + tap + length, :] * kernel[tap : tap + 1, :]
    return summed / (1.0 + jnp.exp(-summed))


def scan_kernel(
    model_width,
    slots,
    accepted,
    live,
    proj_ref,
    inner_cache,
    proj_cache,
    inner_kernel,
    proj_kernel,
    head_ref,
    state_ref,
    *rest,
):
    states_ref, gated_ref, weights_ref, b_ref, joined, joined_bc = rest[-6:]
    request = pl.program_id(0)
    heads, size, state = state_ref.shape[2:]
    inner = heads * size

    @pl.when(request == 0)
    def _():
        weights_ref[...] = jnp.zeros_like(weights_ref)

    block = proj_ref[...].astype(F32)
    tail = 2 * inner + 2 * state
    square = block[:, tail + heads : tail + heads + 1]
    scale = lax.rsqrt(square / model_width + EPSILON)
    gate = block[:, :inner] * scale
    x = conv_silu(
        joined, inner_cache[0, 0].astype(F32), block[:, inner : 2 * inner] * scale, inner_kernel[0]
    )
    bc = conv_silu(
        joined_bc, proj_cache[0, 0].astype(F32), block[:, 2 * inner : tail] * scale, proj_kernel[0]
    )
    b_val = bc[:, :state]
    c_val = bc[:, state:]
    b_half = b_val.astype(BF16)
    c_half = c_val.astype(BF16)
    raw = block[:, tail : tail + heads] * scale + head_ref[0, 0:1, :]
    delta = jnp.maximum(raw, 0.0) + jnp.log(1.0 + jnp.exp(-jnp.abs(raw)))
    log_decay = -delta * jnp.exp(head_ref[0, 1:2, :])
    decay = jnp.exp(log_decay)
    row = lax.broadcasted_iota(jnp.int32, (S, S), 0)
    column = lax.broadcasted_iota(jnp.int32, (S, S), 1)
    lower = (column <= row).astype(F32)
    cum_log = jnp.dot(lower, log_decay, precision=HIGH, preferred_element_type=F32)
    cum_log_t = dot_nt(
        (
            lax.broadcasted_iota(jnp.int32, (heads, heads), 0)
            == lax.broadcasted_iota(jnp.int32, (heads, heads), 1)
        ).astype(F32),
        cum_log,
        precision=HIGH,
    )
    taken = accepted[request]
    alive = live[request].astype(F32)
    steps = lax.broadcasted_iota(jnp.int32, (S, heads), 0)
    cum_end = jnp.sum(jnp.where(steps < taken, log_decay, 0.0), axis=0, keepdims=True)
    keep = jnp.where(steps < taken, jnp.exp(jnp.minimum(cum_end - cum_log, 0.0)), 0.0) * alive
    spread = (
        lax.broadcasted_iota(jnp.int32, (heads, inner), 1) // size
        == lax.broadcasted_iota(jnp.int32, (heads, inner), 0)
    ).astype(F32)
    stacked = jnp.concatenate([delta, jnp.exp(cum_log), keep], axis=0)
    wide = jnp.dot(stacked, spread, precision=HIGH, preferred_element_type=F32)
    skip_wide = jnp.dot(head_ref[0], spread, precision=HIGH, preferred_element_type=F32)[2:3]
    dx = wide[:S] * x
    dx_half = dx.astype(BF16)

    slot = slots[request]
    weights_ref[slot, :, :inner] = (wide[2 * S :] * dx).astype(BF16)
    end_row = jnp.broadcast_to(jnp.exp(cum_end) * alive, (S, heads))
    weights_ref[slot, :, inner:] = jnp.concatenate(
        [end_row, jnp.zeros((S, LANES - heads), F32)], axis=1
    ).astype(BF16)
    b_ref[0] = b_half

    start = state_ref[0, 0].reshape(inner, state)
    y = wide[S : 2 * S] * dot_nt(c_half, start.astype(BF16)) + skip_wide * x
    score = dot_nt(c_half, b_half)
    parts = []
    for head in range(heads):
        gap = jnp.minimum(cum_log[:, head : head + 1] - cum_log_t[head : head + 1, :], 0.0)
        weight = jnp.where(column <= row, jnp.exp(gap) * score, 0.0)
        parts.append(
            jnp.dot(
                weight.astype(BF16),
                dx_half[:, head * size : (head + 1) * size],
                preferred_element_type=F32,
            )
        )
    y = y + jnp.concatenate(parts, axis=1)
    gated_ref[...] = (y * (gate / (1.0 + jnp.exp(-gate)))).astype(BF16)

    dx_t = dx.T
    for head in range(heads):
        carried = state_ref[0, 0, head]
        for step in range(S):
            carried = (
                decay[step : step + 1, head : head + 1] * carried
                + dx_t[head * size : (head + 1) * size, step : step + 1] * b_val[step : step + 1, :]
            )
            states_ref[0, 0, step, head] = carried.astype(BF16)


def scan_layer(
    layer, model_width, count, slots, accepted, live, proj, inner_cache, proj_cache,
    inner_kernel, proj_kernel, head_rows, state_cache, states,
):
    layers, requests, heads, size, state = state_cache.shape
    inner = heads * size
    width = proj.shape[1]
    prefix = inner_cache.shape[2]
    taps = inner_kernel.shape[1]
    in_specs = [
        pl.BlockSpec((S, width), lambda q, *_: (q, 0)),
        pl.BlockSpec((1, 1, prefix, inner), lambda q, *_: (layer, q, 0, 0)),
        pl.BlockSpec((1, 1, prefix, 2 * state), lambda q, *_: (layer, q, 0, 0)),
        pl.BlockSpec((1, taps, inner), lambda q, *_: (layer, 0, 0)),
        pl.BlockSpec((1, taps, 2 * state), lambda q, *_: (layer, 0, 0)),
        pl.BlockSpec((1, 8, heads), lambda q, *_: (layer, 0, 0)),
        pl.BlockSpec((1, 1, heads, size, state), lambda q, *_: (layer, q, 0, 0, 0)),
    ]
    operands = [
        slots, accepted, live, proj, inner_cache, proj_cache, inner_kernel, proj_kernel,
        head_rows, state_cache,
    ]
    aliases = {}
    if states is not None:
        in_specs.append(pl.BlockSpec(memory_space=pl.ANY))
        aliases = {len(operands): 0}
        operands.append(states)
    return pl.pallas_call(
        functools.partial(scan_kernel, model_width),
        grid_spec=pltpu.PrefetchScalarGridSpec(
            num_scalar_prefetch=3,
            grid=(requests,),
            in_specs=in_specs,
            out_specs=[
                pl.BlockSpec((1, 1, S, heads, size, state), lambda q, *_: (layer, q, 0, 0, 0, 0)),
                pl.BlockSpec((S, inner), lambda q, *_: (q, 0)),
                pl.BlockSpec((count * SEND_CAP, S, inner + LANES), lambda q, *_: (0, 0, 0)),
                pl.BlockSpec((1, S, state), lambda q, *_: (q, 0, 0)),
            ],
            scratch_shapes=[
                pltpu.VMEM((8 + S, inner), F32),
                pltpu.VMEM((8 + S, 2 * state), F32),
            ],
        ),
        out_shape=[
            jax.ShapeDtypeStruct((layers, requests, S, heads, size, state), BF16),
            jax.ShapeDtypeStruct((requests * S, inner), BF16),
            jax.ShapeDtypeStruct((count * SEND_CAP, S, inner + LANES), BF16),
            jax.ShapeDtypeStruct((requests, S, state), BF16),
        ],
        input_output_aliases=aliases,
        compiler_params=pltpu.CompilerParams(vmem_limit_bytes=VMEM_LIMIT),
        cost_estimate=pl.CostEstimate(
            flops=requests * S * inner * state * 8,
            bytes_accessed=requests * S * inner * state * 3,
            transcendentals=0,
        ),
    )(*operands)


def owned_kernel(heads, size, mine, weights_ref, b_ref, *rest):
    start_refs, out_ref = rest[:-1], rest[-1]
    slot, layer = pl.program_id(0), pl.program_id(1)
    request = mine[slot]
    count = len(start_refs)
    column = lax.axis_index("col")
    inner = heads * size
    state = out_ref.shape[-1]
    b_half = b_ref[0, request]
    spread = (
        lax.broadcasted_iota(jnp.int32, (inner, heads), 0) // size
        == lax.broadcasted_iota(jnp.int32, (inner, heads), 1)
    ).astype(F32)
    for offset in range(count):
        source = lax.rem(column - offset + count, count)
        message = weights_ref[0, offset, 0]
        added = dot_tn(message[:, :inner], b_half)
        ends = message[0:1, inner : inner + heads].astype(F32)
        end = jnp.sum(spread * ends, axis=1, keepdims=True)
        start = start_refs[offset][0, 0].astype(F32).reshape(inner, state)
        out_ref[0, 0, 0, 0, pl.ds(source * heads, heads)] = (
            (end * start + added).astype(BF16).reshape(heads, size, state)
        )


def owned_states(mine, weights, b_all, starts, layers, heads, size, state):
    count = len(starts)
    requests = b_all.shape[1]
    width = weights.shape[-1]
    return pl.pallas_call(
        functools.partial(owned_kernel, heads, size),
        grid_spec=pltpu.PrefetchScalarGridSpec(
            num_scalar_prefetch=1,
            grid=(SEND_CAP, layers),
            in_specs=[
                pl.BlockSpec((1, count, 1, S, width), lambda r, l, *_: (l, 0, r, 0, 0)),
                pl.BlockSpec((1, requests, S, state), lambda r, l, *_: (l, 0, 0, 0)),
            ]
            + [pl.BlockSpec((1, 1, heads, size, state), lambda r, l, *_: (r, l, 0, 0, 0))] * count,
            out_specs=pl.BlockSpec(
                (1, 1, 1, 1, heads * count, size, state), lambda r, l, *_: (0, 0, r, l, 0, 0, 0)
            ),
        ),
        out_shape=jax.ShapeDtypeStruct(
            (1, 1, SEND_CAP, layers, heads * count, size, state), BF16
        ),
        compiler_params=pltpu.CompilerParams(vmem_limit_bytes=VMEM_LIMIT),
    )(mine, weights, b_all, *starts)


def rotate(array, offset, count):
    return lax.ppermute(array, "col", [(c, (c + offset) % count) for c in range(count)])


def local(
    hidden_states,
    input_gain,
    inner_weight,
    proj_weight,
    step_weight,
    inner_kernel,
    proj_kernel,
    step_bias,
    decay_log,
    skip_gain,
    norm_gain,
    out_weight,
    inner_cache,
    proj_cache,
    state_cache,
    accepted,
    owners,
    tenant_ranges,
):
    layers = inner_weight.shape[0]
    row_width = inner_weight.shape[1]
    inner = inner_weight.shape[3]
    heads = step_weight.shape[2]
    size = inner // heads
    state = proj_weight.shape[2] // 2
    requests = state_cache.shape[1]
    row_count = lax.axis_size("row")
    col_count = lax.axis_size("col")
    model_width = row_width * row_count
    inner_width = inner * col_count
    me = lax.axis_index("col")
    ids = jnp.arange(requests, dtype=jnp.int32)
    request_ids = lax.axis_index("row") * requests + ids
    live = jnp.any(
        (request_ids[:, None] >= tenant_ranges[None, :, 0])
        & (request_ids[:, None] < tenant_ranges[None, :, 1]),
        axis=1,
    ).astype(jnp.int32)
    earlier = (owners[:, None] == owners[None, :]) & (ids[None, :] < ids[:, None])
    ranks = jnp.sum(earlier.astype(jnp.int32), axis=1)
    slots = lax.rem(owners - me + col_count, col_count) * SEND_CAP + ranks
    grid = jnp.arange(col_count * SEND_CAP, dtype=jnp.int32)
    slot_requests = jnp.sum(
        jnp.where(slots[None, :] == grid[:, None], ids[None, :], 0), axis=1
    ).astype(jnp.int32)
    mine = slot_requests[:SEND_CAP]

    picked = pick_states(slot_requests, state_cache, col_count)
    starts = [picked[0]] + [
        rotate(picked[offset], offset, col_count) for offset in range(1, col_count)
    ]

    head_rows = jnp.pad(
        jnp.stack([step_bias, decay_log, skip_gain], axis=1), ((0, 0), (0, 5), (0, 0))
    )
    hidden = hidden_states
    states = None
    weight_layers = []
    b_layers = []
    for layer in range(layers):
        tokens = lax.all_gather(hidden, "col", axis=0, tiled=True).astype(F32)
        scaled = (tokens * input_gain[layer]).astype(BF16)
        square = jnp.sum(tokens * tokens, axis=1, keepdims=True)
        weight = inner_weight[layer].reshape(row_width, 2 * inner)
        partial = jnp.concatenate(
            [
                jnp.dot(scaled, weight, preferred_element_type=F32),
                jnp.dot(scaled, proj_weight[layer], preferred_element_type=F32),
                jnp.dot(scaled, step_weight[layer], preferred_element_type=F32),
                square,
                jnp.zeros((tokens.shape[0], LANES - heads - 1), F32),
            ],
            axis=1,
        )
        proj = lax.psum_scatter(partial, "row", scatter_dimension=0, tiled=True)
        states, gated, sent, b_half = scan_layer(
            layer, model_width, col_count, slots, accepted, live, proj, inner_cache, proj_cache,
            inner_kernel, proj_kernel, head_rows, state_cache, states,
        )
        weight_layers.append(sent)
        b_layers.append(b_half)
        gathered = lax.all_gather(gated, "row", axis=0, tiled=True).astype(F32)
        gate_square = jnp.sum(gathered * gathered, axis=1, keepdims=True)
        partial_out = jnp.dot(
            (gathered * norm_gain[layer]).astype(BF16),
            out_weight[layer],
            preferred_element_type=F32,
        )
        message = jnp.concatenate(
            [partial_out, jnp.broadcast_to(gate_square, (gathered.shape[0], LANES))], axis=1
        ).astype(BF16)
        total = lax.psum_scatter(message, "col", scatter_dimension=0, tiled=True).astype(F32)
        factor = lax.rsqrt(total[:, row_width : row_width + 1] / inner_width + EPSILON)
        hidden = (hidden.astype(F32) + total[:, :row_width] * factor).astype(BF16)

    sent = jnp.stack(weight_layers).reshape(layers, col_count, SEND_CAP, S, inner + LANES)
    received = [sent[:, 0]] + [
        rotate(sent[:, offset], offset, col_count) for offset in range(1, col_count)
    ]
    owned = owned_states(
        mine, jnp.stack(received, axis=1), jnp.stack(b_layers), starts, layers, heads, size, state
    )
    return (hidden, states, owned)


def solution(mesh):
    placed = (
        P("col", "row"),
        P(None, "row"),
        P(None, "row", None, "col"),
        P(None, "row", None),
        P(None, "row", "col"),
        P(None, None, "col"),
        P(),
        P(None, "col"),
        P(None, "col"),
        P(None, "col"),
        P(None, "col"),
        P(None, "col", "row"),
        P(None, "row", None, "col"),
        P(None, "row", None, None),
        P(None, "row", "col", None, None),
        P("row"),
        P("row"),
        P(),
    )
    return jax.shard_map(
        local,
        mesh=mesh,
        in_specs=placed,
        out_specs=(
            P("col", "row"),
            P(None, "row", None, "col", None, None),
            P("row", "col", None, None, None, None, None),
        ),
        check_vma=False,
    )
```

time: 863 us -> 426 us (0.49)
  matrix products: 213 us -> 6.29 us
  other arithmetic: 147 us -> 3 us
  blocking collectives: 196 us -> 78.2 us
  Pallas kernels: 0 us -> 48.5 us
  local copies, waits for them, and re-layouts: 78.6 us -> 32.5 us
  starting transfers between devices: 6.02 us -> 43.6 us
    dot_general x42 -> x8, matrix products: 213 us -> 6.29 us  [the longest x2 2.65 us: local(): jnp.dot(scaled, weight, preferred_element_type=F32)]
    reduce_scatter x8 -> x2, waiting for transfers between devices: 202 us -> 63 us  [local(): proj = lax.psum_scatter(partial, 'row', scatter_dimension=0, tiled=True)]
    psum x2 -> x0, blocking collectives: 106 us -> none  [local(): gate_square = lax.psum(jnp.sum(gated_raw * gated_raw, axis=1), 'col')]
    dynamic_update_slice x64 -> x0, other arithmetic: 95.7 us -> none  [ssm_scan(): last_state, (outputs, states) = lax.scan(advance, start_state, time_major)]
    unnamed x8 -> x6, waiting for transfers between devices: 0.13 us -> 84.5 us
    ppermute x0 -> x14, waiting for transfers between devices: none -> 51.1 us  [rotate(): lax.ppermute(array, 'col', [(c, (c + offset) % count) for c in range(coun...]
    pallas_call x0 -> x4, Pallas kernels: none -> 48.5 us  [the longest x2 39.3 us: scan_layer(): pl.pallas_call(functools.partial(scan_kernel, model_width), grid_spec=plt...]
    ppermute x0 -> x14, starting transfers between devices: none -> 43.5 us  [rotate(): lax.ppermute(array, 'col', [(c, (c + offset) % count) for c in range(coun...]
  transfers between devices with their start and end apart: 9 -> 18, of which waited for: 5 -> 8; matrix products, arithmetic and copies ran while one was open for 9% -> 2% of each run, Pallas kernels for 0% -> 7%
where the time goes in v1:
time: 426 us; the launch traced here: 425 us
  waiting for transfers between devices  199 us (47%)
  blocking collectives  78.2 us (18%)
  Pallas kernels  48.5 us (11%)
  starting transfers between devices  43.6 us (10%)
  local copies, waits for them, and re-layouts  32.5 us (8%)
  between operations  14.3 us (3%)
  matrix products  6.29 us (1%)
    unnamed x6, waiting for transfers between devices  84.5 us
    all_gather x2, blocking collectives, local(): tokens = lax.all_gather(hidden, 'col', axis=0, tiled=True).astype(F32)  64.7 us
    reduce_scatter x2, waiting for transfers between devices, local(): proj = lax.psum_scatter(partial, 'row', scatter_dimension=0, tiled=True)  63 us
    ppermute x14, waiting for transfers between devices, rotate(): lax.ppermute(array, 'col', [(c, (c + offset) % count) for c in range(coun...  51.1 us
    ppermute x14, starting transfers between devices, rotate(): lax.ppermute(array, 'col', [(c, (c + offset) % count) for c in range(coun...  43.5 us
    pallas_call x2, Pallas kernels, scan_layer(): pl.pallas_call(functools.partial(scan_kernel, model_width), grid_spec=plt...  39.3 us
    unnamed x78, local copies, waits for them, and re-layouts  21.6 us
    all_gather x2, blocking collectives, local(): gathered = lax.all_gather(gated, 'row', axis=0, tiled=True).astype(F32)  13.4 us
  transfers between devices with their start and end apart: 18, of which 8 were waited for; matrix products, arithmetic and copies ran while one was open for 2% of the time, Pallas kernels for 7%

profile of v1, /device:TPU:0, one launch (start us, length us, event | category | flops | bytes accessed | tf_op | source)
XLA Modules:
  0.0 425.0 jit_solution(12504483677953248940)
XLA Ops:
  7.2 33.2 %all_gather.12 = bf16[512,512]{1,0:T(8,128)(2,1)S(1)} all-gather(bf16[64,512]{1,0:T(8,128)(2,1)} %param.18), channel_id=1, replica_groups=mesh['row'=4,'col'=8] {'col'}, dimensions={0}, use_global_device_ids=true | all-gather | bytes 589824 | tf_op jit(solution)/shard_map/all_gather | solution.py:356
  40.4 0.8 fusion.66
  41.2 3.5 fusion.64
  44.7 0.2 copy.118
  44.9 0.2 fusion.1
  45.1 0.7 fusion.26
  46.0 0.3 fusion.24
  46.3 0.3 fusion.22
  46.8 2.3 concatenate.15
  49.3 0.5 copy-done.22
  50.0 0.2 convert_reduce_fusion
  50.3 36.5 %reduce-scatter.9.cloned.1.call-done.proj_ref = f32[128,1408]{1,0:T(8,128)} async-done(((f32[512,1408]{1,0:T(8,128)}), f32[128,1408]{1,0:T(8,128)}) %reduce-scatter.9.cloned.1.call-update) | async-done | bytes 720912 | tf_op jit(solution)/shard_map/reduce_scatter | solution.py:370
  86.8 2.2 copy-done
  89.0 1.1 copy-done.2
  90.1 19.7 %shard_map.193 = (bf16[2,8,16,8,64,128]{5,4,3,2,1,0:T(8,128)(2,1)}, bf16[128,512]{1,0:T(8,128)(2,1)S(1)}, bf16[16,16,640]{2,1,0:T(8,128)(2,1)S(1)}, bf16[8,16,128]{2,1,0:T(8,128)(2,1)S(1)}) custom-call(s32[8]{0:T(128)S(1)} %fusion.57.slots, s32[8]{0:T(128)S(1)} %copy-done.6, s32[8]{0:T(128)S(1)} %convert_element_type.54.live, f32[128,1408]{1,0:T(8,128)S(1)} %copy-done.2, ...), custom_call_target="tpu_custom_call" | custom-call | flops 67108864 | bytes 25165824 | tf_op jit(solution)/shard_map/pallas_call | solution.py:208
  109.8 6.8 %all_gather.13 = bf16[512,512]{1,0:T(8,128)(2,1)S(1)} all-gather(bf16[128,512]{1,0:T(8,128)(2,1)S(1)} %get-tuple-element.19), channel_id=1, replica_groups=mesh['row'=4,'col'=8] {'row'}, dimensions={0}, use_global_device_ids=true | all-gather | bytes 655360 | tf_op jit(solution)/shard_map/all_gather | solution.py:377
  116.7 0.5 convolution_convert_fusion.1
  117.3 1.1 copy.114
  118.6 1.2 copy.119
  119.9 61.2 %reduce-scatter.13.cloned.1.call-done = bf16[64,640]{1,0:T(8,128)(2,1)} async-done(((bf16[512,640]{1,0:T(8,128)(2,1)}), bf16[64,640]{1,0:T(8,128)(2,1)}) %reduce-scatter.13.cloned.1.call-update) | async-done | bytes 81936
  181.1 1.0 copy.115
  182.3 31.5 %all_gather.14 = bf16[512,512]{1,0:T(8,128)(2,1)S(1)} all-gather(bf16[64,512]{1,0:T(8,128)(2,1)S(1)} %copy.96), channel_id=1, replica_groups=mesh['row'=4,'col'=8] {'col'}, dimensions={0}, use_global_device_ids=true | all-gather | bytes 589824 | tf_op jit(solution)/shard_map/all_gather | solution.py:356
  213.8 1.1 fusion.18
  214.9 1.0 fusion.16
  216.1 1.9 fusion.20
  218.2 3.8 concatenate.17
  222.2 3.9 shard_map.195
  226.1 0.8 copy-done.7
  226.9 0.8 copy-done.8
  227.7 0.8 copy-done.9
  228.5 0.8 copy-done.10
  229.3 1.9 collective-permute-start.11
  231.1 26.5 %reduce-scatter.11.cloned.1.call-done.proj_ref = f32[128,1408]{1,0:T(8,128)} async-done(((f32[512,1408]{1,0:T(8,128)}), f32[128,1408]{1,0:T(8,128)}) %reduce-scatter.11.cloned.1.call-update) | async-done | bytes 720912 | tf_op jit(solution)/shard_map/reduce_scatter | solution.py:370
  257.6 2.2 copy-done.1
  259.8 1.1 copy-done.3
  260.9 19.7 %shard_map.194 = (bf16[2,8,16,8,64,128]{5,4,3,2,1,0:T(8,128)(2,1)}, bf16[128,512]{1,0:T(8,128)(2,1)S(1)}, bf16[16,16,640]{2,1,0:T(8,128)(2,1)S(1)}, bf16[8,16,128]{2,1,0:T(8,128)(2,1)S(1)}) custom-call(s32[8]{0:T(128)S(1)} %fusion.57.slots, s32[8]{0:T(128)S(1)} %copy-done.6, s32[8]{0:T(128)S(1)} %convert_element_type.54.live, ...), custom_call_target="tpu_custom_call", output_to_operand_aliasing={{0}: (10, {})} | custom-call | flops 67108864 | bytes 25165824 | tf_op jit(solution)/shard_map/pallas_call | solution.py:208
  280.6 0.8 fusion.43
  281.4 1.5 collective-permute-start
  282.9 1.5 collective-permute-start.1
  284.4 2.4 collective-permute-start.2
  286.8 6.7 %all_gather.15 = bf16[512,512]{1,0:T(8,128)(2,1)S(1)} all-gather(bf16[128,512]{1,0:T(8,128)(2,1)S(1)} %get-tuple-element.21), channel_id=1, replica_groups=mesh['row'=4,'col'=8] {'row'}, dimensions={0}, use_global_device_ids=true | all-gather | bytes 655360 | tf_op jit(solution)/shard_map/all_gather | solution.py:377
  293.7 0.5 convolution_convert_fusion
  294.2 0.9 pad_maximum_fusion.1
  295.1 2.2 copy.116
  297.3 1.5 collective-permute-start.3
  298.8 0.9 bitcast_dynamic-update-slice_fusion.5
  299.7 0.6 copy-done.18
  300.3 2.4 collective-permute-start.4
  302.7 0.9 bitcast_dynamic-update-slice_fusion.4
  303.7 1.5 collective-permute-start.5
  305.1 0.9 bitcast_dynamic-update-slice_fusion.3
  306.1 1.5 collective-permute-start.6
  307.6 0.6 collective-permute-start.12
  308.2 1.4 collective-permute-start.13
  309.6 1.1 collective-permute-start.7
  310.7 0.3 collective-permute-done.5
  311.0 26.2 %collective-permute-start.8 = (bf16[2,2,8,64,128]{4,3,2,1,0:T(8,128)(2,1)}, bf16[2,2,8,64,128]{4,3,2,1,0:T(8,128)(2,1)S(1)}, u32[]{:S(2)}, u32[]{:S(2)}) collective-permute-start(bf16[2,2,8,64,128]{4,3,2,1,0:T(8,128)(2,1)} %copy-done.7), channel_id=1, source_target_pairs={{0,2},{1,3},{2,4},{3,5},{4,6},{5,7},{6,0},{7,1},{8,10},{9,11},{10,... | collective-permute-start | bytes 1572872 | tf_op jit(solution)/shard_map/ppermute | solution.py:292
  337.3 18.4 %collective-permute-done.7.rest_1_ = bf16[2,2,8,64,128]{4,3,2,1,0:T(8,128)(2,1)S(1)} collective-permute-done((bf16[2,2,8,64,128]{4,3,2,1,0:T(8,128)(2,1)}, bf16[2,2,8,64,128]{4,3,2,1,0:T(8,128)(2,1)S(1)}, u32[]{:S(2)}, u32[]{:S(2)}) %collective-permute-start.7) | collective-permute-done | bytes 524320 | tf_op jit(solution)/shard_map/ppermute | solution.py:292
  355.7 0.4 collective-permute-done.8.rest_2_
  356.1 31.9 %collective-permute-done.9.rest_3_ = bf16[2,2,8,64,128]{4,3,2,1,0:T(8,128)(2,1)S(1)} collective-permute-done((bf16[2,2,8,64,128]{4,3,2,1,0:T(8,128)(2,1)S(1)}, bf16[2,2,8,64,128]{4,3,2,1,0:T(8,128)(2,1)S(1)}, u32[]{:S(2)}, u32[]{:S(2)}) %collective-permute-start.9) | collective-permute-done | bytes 524320 | tf_op jit(solution)/shard_map/ppermute | solution.py:292
  388.0 5.3 %shard_map.196 = bf16[1,1,2,2,64,64,128]{6,5,4,3,2,1,0:T(8,128)(2,1)} custom-call(s32[2]{0:T(128)S(1)} %bitcast.104, bf16[2,8,2,16,640]{4,3,2,1,0:T(8,128)(2,1)S(1)} %bitcast_dynamic-update-slice_fusion.6.weights_ref, bf16[2,8,16,128]{3,2,1,0:T(8,128)(2,1)S(1)} %pad_maximum_fusion.3.b_ref, bf16[2,2,8,64,128]{4,3,2,1,0:T(8,128)(2,1)S(1)} %get-tuple-element.27.rest_0_, ...), custom_call_target="tpu_custom_call" | custom-call | tf_op jit(solution)/shard_map/pallas_call | solution.py:270
  393.4 23.2 %reduce-scatter.15.cloned.1.call-done = bf16[64,640]{1,0:T(8,128)(2,1)} async-done(((bf16[512,640]{1,0:T(8,128)(2,1)}), bf16[64,640]{1,0:T(8,128)(2,1)}) %reduce-scatter.15.cloned.1.call-update) | async-done | bytes 81936
  416.6 1.0 copy.117
  417.7 0.7 copy.109
  (105 shorter events, 2.2 us)
Async XLA Ops:
  7.2 79.6 %reduce-scatter.9.cloned.1.call-start = ((), (), s32[]{:S(2)}) async-start(), calls=%async_computation.4 | async-start | bytes 3604480 | tf_op jit(solution)/shard_map/reduce_scatter | solution.py:370
  44.9 1.0 copy-start.12
  45.1 1.2 copy-start.29
  49.1 0.7 copy-start.22
  49.1 0.8 copy-start.19
  49.1 0.9 copy-start.20
  49.1 0.9 copy-start.23
  49.1 0.9 copy-start.24
  49.1 0.9 copy-start.25
  49.1 0.9 copy-start.26
  49.1 1.1 copy-start.21
  49.2 37.6 %copy-start.4 = (f32[2,4,512]{2,1,0:T(4,128)S(1)}, f32[2,4,512]{2,1,0:T(4,128)}, u32[]{:S(2)}) copy-start(f32[2,4,512]{2,1,0:T(4,128)} %inner_kernel.3) | copy-start | bytes 49156
  49.2 37.6 %copy-start.5 = (f32[2,4,256]{2,1,0:T(4,128)S(1)}, f32[2,4,256]{2,1,0:T(4,128)}, u32[]{:S(2)}) copy-start(f32[2,4,256]{2,1,0:T(4,128)} %proj_kernel.3) | copy-start | bytes 24580
  49.2 37.6 %copy-start.6 = (s32[8]{0:T(128)S(1)}, s32[8]{0:T(128)}, u32[]{:S(2)}) copy-start(s32[8]{0:T(128)} %accepted.3) | copy-start | bytes 100
  49.2 131.8 %reduce-scatter.13.cloned.1.call-start = ((), (), s32[]{:S(2)}) async-start(), calls=%async_computation.6 | async-start | bytes 737280
  86.8 2.2 copy-start
  89.0 1.1 copy-start.2
  90.1 26.6 %copy-start.27 = (bf16[2,512,512]{2,1,0:T(8,128)(2,1)S(1)}, bf16[2,512,512]{2,1,0:T(8,128)(2,1)}, u32[]{:S(2)}) copy-start(bf16[2,512,512]{2,1,0:T(8,128)(2,1)} %param.29) | copy-start | bytes 3145732
  117.2 1.3 copy-start.14
  117.2 1.4 copy-start.11
  118.4 139.2 %reduce-scatter.11.cloned.1.call-start = ((), (), s32[]{:S(2)}) async-start(), calls=%async_computation.5 | async-start | bytes 3604480 | tf_op jit(solution)/shard_map/reduce_scatter | solution.py:370
  118.6 95.2 %copy-start.13 = (bf16[2,512,256]{2,1,0:T(8,128)(2,1)S(1)}, bf16[2,512,256]{2,1,0:T(8,128)(2,1)}, u32[]{:S(2)}) copy-start(bf16[2,512,256]{2,1,0:T(8,128)(2,1)} %param.21) | copy-start | bytes 1572868
  119.9 95.1 %copy-start.30 = (bf16[2,512,8]{1,2,0:T(8,128)(2,1)S(1)}, bf16[2,512,8]{1,2,0:T(8,128)(2,1)}, u32[]{:S(2)}) copy-start(bf16[2,512,8]{1,2,0:T(8,128)(2,1)} %param.22) | copy-start | bytes 49156
  222.0 194.5 %reduce-scatter.15.cloned.1.call-start = ((), (), s32[]{:S(2)}) async-start(), calls=%async_computation.7 | async-start | bytes 737280
  226.1 0.8 copy-start.7
  226.9 0.8 copy-start.8
  227.7 0.8 copy-start.9
  228.5 0.8 copy-start.10
  229.3 78.3 %collective-permute-start.10 = (bf16[2,2,8,64,128]{4,3,2,1,0:T(8,128)(2,1)}, bf16[2,2,8,64,128]{4,3,2,1,0:T(8,128)(2,1)S(1)}, u32[]{:S(2)}, u32[]{:S(2)}) collective-permute-start(bf16[2,2,8,64,128]{4,3,2,1,0:T(8,128)(2,1)} %get-tuple-element.31), channel_id=1, source_target_pairs={{0,4},{1,5},{2,6},{3,7},{4,0},{5,1},{6,2},{7,3},{8,12},{9,13},{10,... | collective-permute-start | bytes 1572872 | tf_op jit(solution)/shard_map/ppermute | solution.py:292
  229.3 78.9 %collective-permute-start.11 = (bf16[2,2,8,64,128]{4,3,2,1,0:T(8,128)(2,1)}, bf16[2,2,8,64,128]{4,3,2,1,0:T(8,128)(2,1)S(1)}, u32[]{:S(2)}, u32[]{:S(2)}) collective-permute-start(bf16[2,2,8,64,128]{4,3,2,1,0:T(8,128)(2,1)} %get-tuple-element.32), channel_id=1, source_target_pairs={{0,5},{1,6},{2,7},{3,0},{4,1},{5,2},{6,3},{7,4},{8,13},{9,14},{10,... | collective-permute-start | bytes 1572872 | tf_op jit(solution)/shard_map/ppermute | solution.py:292
  257.6 2.2 copy-start.1
  259.8 1.1 copy-start.3
  280.6 13.1 %copy-start.28 = (bf16[2,512,512]{2,1,0:T(8,128)(2,1)S(1)}, bf16[2,512,512]{2,1,0:T(8,128)(2,1)}, u32[]{:S(2)}) copy-start(bf16[2,512,512]{2,1,0:T(8,128)(2,1)} %param.29) | copy-start | bytes 3145732
  281.4 15.9 %collective-permute-start = (bf16[2,2,16,640]{3,2,1,0:T(8,128)(2,1)}, bf16[2,2,16,640]{3,2,1,0:T(8,128)(2,1)}, u32[]{:S(2)}, u32[]{:S(2)}) collective-permute-start(bf16[2,2,16,640]{3,2,1,0:T(8,128)(2,1)} %get-tuple-element.50), channel_id=1, source_target_pairs={{0,1},{1,2},{2,3},{3,4},{4,5},{5,6},{6,7},{7,0},{8,9},{9,10},{10,1... | collective-permute-start | bytes 245768 | tf_op jit(solution)/shard_map/ppermute | solution.py:292
  282.9 16.8 %collective-permute-start.1 = (bf16[2,2,16,640]{3,2,1,0:T(8,128)(2,1)}, bf16[2,2,16,640]{3,2,1,0:T(8,128)(2,1)S(1)}, u32[]{:S(2)}, u32[]{:S(2)}) collective-permute-start(bf16[2,2,16,640]{3,2,1,0:T(8,128)(2,1)} %get-tuple-element.51), channel_id=1, source_target_pairs={{0,2},{1,3},{2,4},{3,5},{4,6},{5,7},{6,0},{7,1},{8,10},{9,11},{10,... | collective-permute-start | bytes 245768 | tf_op jit(solution)/shard_map/ppermute | solution.py:292
  284.4 19.3 %collective-permute-start.2 = (bf16[2,2,16,640]{3,2,1,0:T(8,128)(2,1)}, bf16[2,2,16,640]{3,2,1,0:T(8,128)(2,1)}, u32[]{:S(2)}, u32[]{:S(2)}) collective-permute-start(bf16[2,2,16,640]{3,2,1,0:T(8,128)(2,1)} %get-tuple-element.52), channel_id=1, source_target_pairs={{0,3},{1,4},{2,5},{3,6},{4,7},{5,0},{6,1},{7,2},{8,11},{9,12},{10,... | collective-permute-start | bytes 245768 | tf_op jit(solution)/shard_map/ppermute | solution.py:292
  294.1 3.1 copy-start.17
  294.2 6.2 %copy-start.16 = (bf16[2,2,16,640]{3,2,1,0:T(8,128)(2,1)S(1)}, bf16[2,2,16,640]{3,2,1,0:T(8,128)(2,1)}, u32[]{:S(2)}) copy-start(bf16[2,2,16,640]{3,2,1,0:T(8,128)(2,1)} %get-tuple-element.54) | copy-start | bytes 245764
  294.2 9.5 %copy-start.15 = (bf16[2,2,16,640]{3,2,1,0:T(8,128)(2,1)S(1)}, bf16[2,2,16,640]{3,2,1,0:T(8,128)(2,1)}, u32[]{:S(2)}) copy-start(bf16[2,2,16,640]{3,2,1,0:T(8,128)(2,1)} %get-tuple-element.55) | copy-start | bytes 245764
  297.3 8.8 %collective-permute-start.3 = (bf16[2,2,16,640]{3,2,1,0:T(8,128)(2,1)S(1)}, bf16[2,2,16,640]{3,2,1,0:T(8,128)(2,1)S(1)}, u32[]{:S(2)}, u32[]{:S(2)}) collective-permute-start(bf16[2,2,16,640]{3,2,1,0:T(8,128)(2,1)S(1)} %copy-done.17), channel_id=1, source_target_pairs={{0,4},{1,5},{2,6},{3,7},{4,0},{5,1},{6,2},{7,3},{8,12},{9,13},{10,... | collective-permute-start | bytes 245768 | tf_op jit(solution)/shard_map/ppermute | solution.py:292
  299.7 0.6 copy-start.18
  300.3 9.3 %collective-permute-start.4 = (bf16[2,2,16,640]{3,2,1,0:T(8,128)(2,1)S(1)}, bf16[2,2,16,640]{3,2,1,0:T(8,128)(2,1)S(1)}, u32[]{:S(2)}, u32[]{:S(2)}) collective-permute-start(bf16[2,2,16,640]{3,2,1,0:T(8,128)(2,1)S(1)} %copy-done.16), channel_id=1, source_target_pairs={{0,5},{1,6},{2,7},{3,0},{4,1},{5,2},{6,3},{7,4},{8,13},{9,14},{10,... | collective-permute-start | bytes 245768 | tf_op jit(solution)/shard_map/ppermute | solution.py:292
  303.7 7.3 %collective-permute-start.5 = (bf16[2,2,16,640]{3,2,1,0:T(8,128)(2,1)S(1)}, bf16[2,2,16,640]{3,2,1,0:T(8,128)(2,1)S(1)}, u32[]{:S(2)}, u32[]{:S(2)}) collective-permute-start(bf16[2,2,16,640]{3,2,1,0:T(8,128)(2,1)S(1)} %copy-done.15), channel_id=1, source_target_pairs={{0,6},{1,7},{2,0},{3,1},{4,2},{5,3},{6,4},{7,5},{8,14},{9,15},{10,... | collective-permute-start | bytes 245768 | tf_op jit(solution)/shard_map/ppermute | solution.py:292
  306.1 31.1 %collective-permute-start.6 = (bf16[2,2,16,640]{3,2,1,0:T(8,128)(2,1)S(1)}, bf16[2,2,16,640]{3,2,1,0:T(8,128)(2,1)S(1)}, u32[]{:S(2)}, u32[]{:S(2)}) collective-permute-start(bf16[2,2,16,640]{3,2,1,0:T(8,128)(2,1)S(1)} %get-tuple-element.49), channel_id=1, source_target_pairs={{0,7},{1,0},{2,1},{3,2},{4,3},{5,4},{6,5},{7,6},{8,15},{9,8},{10,9... | collective-permute-start | bytes 245768 | tf_op jit(solution)/shard_map/ppermute | solution.py:292
  307.6 29.7 %collective-permute-start.12 = (bf16[2,2,8,64,128]{4,3,2,1,0:T(8,128)(2,1)}, bf16[2,2,8,64,128]{4,3,2,1,0:T(8,128)(2,1)S(1)}, u32[]{:S(2)}, u32[]{:S(2)}) collective-permute-start(bf16[2,2,8,64,128]{4,3,2,1,0:T(8,128)(2,1)} %copy-done.10), channel_id=1, source_target_pairs={{0,6},{1,7},{2,0},{3,1},{4,2},{5,3},{6,4},{7,5},{8,14},{9,15},{10,... | collective-permute-start | bytes 1572872 | tf_op jit(solution)/shard_map/ppermute | solution.py:292
  308.2 29.1 %collective-permute-start.13 = (bf16[2,2,8,64,128]{4,3,2,1,0:T(8,128)(2,1)}, bf16[2,2,8,64,128]{4,3,2,1,0:T(8,128)(2,1)S(1)}, u32[]{:S(2)}, u32[]{:S(2)}) collective-permute-start(bf16[2,2,8,64,128]{4,3,2,1,0:T(8,128)(2,1)} %copy-done.9), channel_id=1, source_target_pairs={{0,7},{1,0},{2,1},{3,2},{4,3},{5,4},{6,5},{7,6},{8,15},{9,8},{10,9... | collective-permute-start | bytes 1572872 | tf_op jit(solution)/shard_map/ppermute | solution.py:292
  309.6 46.1 %collective-permute-start.7 = (bf16[2,2,8,64,128]{4,3,2,1,0:T(8,128)(2,1)}, bf16[2,2,8,64,128]{4,3,2,1,0:T(8,128)(2,1)S(1)}, u32[]{:S(2)}, u32[]{:S(2)}) collective-permute-start(bf16[2,2,8,64,128]{4,3,2,1,0:T(8,128)(2,1)} %copy-done.8), channel_id=1, source_target_pairs={{0,1},{1,2},{2,3},{3,4},{4,5},{5,6},{6,7},{7,0},{8,9},{9,10},{10,1... | collective-permute-start | bytes 1572872 | tf_op jit(solution)/shard_map/ppermute | solution.py:292
  311.0 45.1 %collective-permute-start.8 = (bf16[2,2,8,64,128]{4,3,2,1,0:T(8,128)(2,1)}, bf16[2,2,8,64,128]{4,3,2,1,0:T(8,128)(2,1)S(1)}, u32[]{:S(2)}, u32[]{:S(2)}) collective-permute-start(bf16[2,2,8,64,128]{4,3,2,1,0:T(8,128)(2,1)} %copy-done.7), channel_id=1, source_target_pairs={{0,2},{1,3},{2,4},{3,5},{4,6},{5,7},{6,0},{7,1},{8,10},{9,11},{10,... | collective-permute-start | bytes 1572872 | tf_op jit(solution)/shard_map/ppermute | solution.py:292
  337.2 50.8 %collective-permute-start.9 = (bf16[2,2,8,64,128]{4,3,2,1,0:T(8,128)(2,1)S(1)}, bf16[2,2,8,64,128]{4,3,2,1,0:T(8,128)(2,1)S(1)}, u32[]{:S(2)}, u32[]{:S(2)}) collective-permute-start(bf16[2,2,8,64,128]{4,3,2,1,0:T(8,128)(2,1)S(1)} %get-tuple-element.30), channel_id=1, source_target_pairs={{0,3},{1,4},{2,5},{3,6},{4,7},{5,0},{6,1},{7,2},{8,11},{9,12},{10,... | collective-permute-start | bytes 1572872 | tf_op jit(solution)/shard_map/ppermute | solution.py:292
Sparse Core Ops, SparseCore 0:
  49.3 37.4 reduce-scatter.8
  118.5 62.4 reduce-scatter.12
  222.2 35.3 reduce-scatter.10
  297.4 119.1 reduce-scatter.14

commit v2 on v1

--- a/solution.py
+++ b/solution.py
@@ -15,6 +15,7 @@
 BF16 = jnp.bfloat16
 HIGH = lax.Precision.HIGHEST
 VMEM_LIMIT = 48 * 1024 * 1024
+SMALL = pl.CostEstimate(flops=1000000, bytes_accessed=1000000, transcendentals=0)
 
 
 def dot_nt(a, b, precision=None):
@@ -230,11 +231,7 @@
         ],
         input_output_aliases=aliases,
         compiler_params=pltpu.CompilerParams(vmem_limit_bytes=VMEM_LIMIT),
-        cost_estimate=pl.CostEstimate(
-            flops=requests * S * inner * state * 8,
-            bytes_accessed=requests * S * inner * state * 3,
-            transcendentals=0,
-        ),
+        cost_estimate=SMALL,
     )(*operands)
 
 
@@ -286,6 +283,283 @@
         ),
         compiler_params=pltpu.CompilerParams(vmem_limit_bytes=VMEM_LIMIT),
     )(mine, weights, b_all, *starts)
+
+
+MESH = pl.DeviceIdType.MESH
+
+
+def greet(count, row_count):
+    column, row = lax.axis_index("col"), lax.axis_index("row")
+    chips = row_count // 2
+    chip, core = lax.div(row, 2), lax.rem(row, 2)
+    barrier = pltpu.get_barrier_semaphore()
+    for offset in range(1, count):
+        pl.semaphore_signal(
+            barrier, inc=1, device_id={"col": lax.rem(column + offset, count)}, device_id_type=MESH
+        )
+    pl.semaphore_signal(
+        barrier, inc=1, device_id={"row": chip * 2 + 1 - core}, device_id_type=MESH
+    )
+    for step in range(1, chips):
+        other = lax.rem(chip + step, chips) * 2 + core
+        pl.semaphore_signal(barrier, inc=1, device_id={"row": other}, device_id_type=MESH)
+    pl.semaphore_wait(barrier, count - 1 + 1 + chips - 1)
+    return column, row, chips, chip, core
+
+
+def push(source, target, send, receive, device):
+    copy = pltpu.make_async_remote_copy(
+        src_ref=source,
+        dst_ref=target,
+        send_sem=send,
+        recv_sem=receive,
+        device_id=device,
+        device_id_type=MESH,
+    )
+    copy.start()
+    return copy
+
+
+def project_kernel(
+    count, row_count, heads, hidden_ref, gain_ref, weight_ref, out_ref,
+    blocks, kept, core_out, core_in, row_out, row_in,
+    gather_send, gather_recv, core_send, core_recv, row_send, row_recv,
+):
+    column, row, chips, chip, core = greet(count, row_count)
+    per_row = count // row_count
+    tokens, depth = hidden_ref.shape
+    width = weight_ref.shape[1]
+    tail = width - LANES
+    sends = []
+    for offset in range(1, count):
+        sends.append(
+            push(
+                hidden_ref, blocks.at[column], gather_send.at[offset], gather_recv.at[column],
+                {"col": lax.rem(column + offset, count)},
+            )
+        )
+    blocks[column] = hidden_ref[...]
+    lane = lax.broadcasted_iota(jnp.int32, (per_row * tokens, LANES), 1)
+
+    def partial(owner):
+        for index in range(per_row):
+            source = owner * per_row + index
+
+            @pl.when(source != column)
+            def _():
+                pltpu.make_async_remote_copy(
+                    src_ref=hidden_ref,
+                    dst_ref=blocks.at[source],
+                    send_sem=gather_send.at[0],
+                    recv_sem=gather_recv.at[source],
+                    device_id={"col": source},
+                    device_id_type=MESH,
+                ).wait_recv()
+
+        block = blocks[pl.ds(owner * per_row, per_row)].reshape(per_row * tokens, depth)
+        block = block.astype(F32)
+        square = jnp.sum(block * block, axis=1, keepdims=True)
+        product = jnp.dot(
+            (block * gain_ref[...]).astype(BF16), weight_ref[...], preferred_element_type=F32
+        )
+        last = product[:, tail:] + jnp.where(lane == heads, square, 0.0)
+        return product[:, :tail], last
+
+    core_copies = []
+    row_copies = []
+
+    def forward(step):
+        core_copies[step].wait_recv()
+        kept[step] = kept[step] + core_in[step].astype(F32)
+        if step < chips - 1:
+            row_out[step] = kept[step].astype(BF16)
+            row_copies.append(
+                push(
+                    row_out.at[step], row_in.at[step], row_send.at[step], row_recv.at[step],
+                    {"row": lax.rem(chip + 1 + step, chips) * 2 + core},
+                )
+            )
+
+    for step in range(chips):
+        target = lax.rem(chip + 1 + step, chips)
+        main, last = partial(target * 2 + 1 - core)
+        core_out[step, :, :tail] = main.astype(BF16)
+        core_out[step, :, tail:] = last.astype(BF16)
+        core_copies.append(
+            push(
+                core_out.at[step], core_in.at[step], core_send.at[step], core_recv.at[step],
+                {"row": chip * 2 + 1 - core},
+            )
+        )
+        if step > 0:
+            forward(step - 1)
+        main, last = partial(target * 2 + core)
+        kept[step, :, :tail] = main
+        kept[step, :, tail:] = last
+    forward(chips - 1)
+    total = kept[chips - 1]
+    for step in range(chips - 1):
+        row_copies[step].wait_recv()
+        total = total + row_in[step].astype(F32)
+    out_ref[...] = total
+    for copy in sends + core_copies + row_copies:
+        copy.wait_send()
+
+
+def project(layer, count, row_count, heads, hidden, gain, weight):
+    tokens, depth = hidden.shape
+    width = weight.shape[1]
+    rows = tokens * (count // row_count)
+    chips = row_count // 2
+    vmem = pl.BlockSpec(memory_space=pltpu.VMEM)
+    return pl.pallas_call(
+        functools.partial(project_kernel, count, row_count, heads),
+        out_shape=jax.ShapeDtypeStruct((rows, width), F32),
+        in_specs=[vmem] * 3,
+        out_specs=vmem,
+        scratch_shapes=[
+            pltpu.VMEM((count, tokens, depth), BF16),
+            pltpu.VMEM((chips, rows, width), F32),
+            pltpu.VMEM((chips, rows, width), BF16),
+            pltpu.VMEM((chips, rows, width), BF16),
+            pltpu.VMEM((chips, rows, width), BF16),
+            pltpu.VMEM((chips, rows, width), BF16),
+            pltpu.SemaphoreType.DMA((count,)),
+            pltpu.SemaphoreType.DMA((count,)),
+            pltpu.SemaphoreType.DMA((chips,)),
+            pltpu.SemaphoreType.DMA((chips,)),
+            pltpu.SemaphoreType.DMA((chips,)),
+            pltpu.SemaphoreType.DMA((chips,)),
+        ],
+        compiler_params=pltpu.CompilerParams(
+            collective_id=2 * layer, has_side_effects=True, vmem_limit_bytes=VMEM_LIMIT
+        ),
+        cost_estimate=SMALL,
+    )(hidden, gain, weight)
+
+
+def output_kernel(
+    count, row_count, inner_width, gated_ref, gain_ref, weight_ref, hidden_ref, sent_ref,
+    out_ref, received_ref,
+    groups, outbox, inbox, taken,
+    row_send, row_recv, relay_send, relay_recv, sum_send, sum_recv, state_send, state_recv,
+):
+    column, row, chips, chip, core = greet(count, row_count)
+    per_row = count // row_count
+    rows, inner = gated_ref.shape
+    tokens, depth = hidden_ref.shape
+    peer = {"row": chip * 2 + 1 - core}
+    near = [push(gated_ref, groups.at[1], row_send.at[0], row_recv.at[0], peer)]
+    for step in range(1, chips):
+        near.append(
+            push(
+                gated_ref, groups.at[2 * step], row_send.at[step], row_recv.at[step],
+                {"row": lax.rem(chip - step + chips, chips) * 2 + core},
+            )
+        )
+    state_copies = []
+
+    def process(group, owner):
+        value = group.astype(F32)
+        square = jnp.sum(value * value, axis=1, keepdims=True)
+        product = jnp.dot(
+            (value * gain_ref[...]).astype(BF16), weight_ref[...], preferred_element_type=F32
+        )
+        product = product.astype(BF16).reshape(per_row, tokens, depth)
+        square = jnp.broadcast_to(square, (rows, LANES)).astype(BF16)
+        square = square.reshape(per_row, tokens, LANES)
+        for index in range(per_row):
+            target = owner * per_row + index
+            outbox[target, :, :depth] = product[index]
+            outbox[target, :, depth:] = square[index]
+
+            @pl.when(target != column)
+            def _():
+                push(
+                    outbox.at[target], inbox.at[column], sum_send.at[target], sum_recv.at[column],
+                    {"col": target},
+                )
+
+    process(gated_ref[...], row)
+    near[0].wait_recv()
+    process(groups[1], chip * 2 + 1 - core)
+    relays = []
+    for step in range(1, chips):
+        near[step].wait_recv()
+        relays.append(
+            push(
+                groups.at[2 * step], groups.at[2 * step + 1], relay_send.at[step],
+                relay_recv.at[step], peer,
+            )
+        )
+        process(groups[2 * step], lax.rem(chip + step, chips) * 2 + core)
+    for step in range(1, chips):
+        relays[step - 1].wait_recv()
+        process(groups[2 * step + 1], lax.rem(chip + step, chips) * 2 + 1 - core)
+    for offset in range(1, count):
+        state_copies.append(
+            push(
+                sent_ref.at[offset], taken.at[offset], state_send.at[offset],
+                state_recv.at[offset], {"col": lax.rem(column + offset, count)},
+            )
+        )
+    received_ref[0] = sent_ref[0]
+    total = outbox[column].astype(F32)
+    for offset in range(1, count):
+        source = lax.rem(column + offset, count)
+        arrival = pltpu.make_async_remote_copy(
+            src_ref=outbox.at[source],
+            dst_ref=inbox.at[source],
+            send_sem=sum_send.at[source],
+            recv_sem=sum_recv.at[source],
+            device_id={"col": source},
+            device_id_type=MESH,
+        )
+        arrival.wait_recv()
+        total = total + inbox[source].astype(F32)
+        arrival.wait_send()
+    factor = lax.rsqrt(total[:, depth : depth + 1] / inner_width + EPSILON)
+    out_ref[...] = (hidden_ref[...].astype(F32) + total[:, :depth] * factor).astype(BF16)
+    for offset in range(1, count):
+        state_copies[offset - 1].wait()
+        received_ref[offset] = taken[offset]
+    for copy in near + relays:
+        copy.wait_send()
+
+
+def output(layer, count, row_count, inner_width, gated, gain, weight, hidden, sent):
+    tokens, depth = hidden.shape
+    rows, inner = gated.shape
+    chips = row_count // 2
+    vmem = pl.BlockSpec(memory_space=pltpu.VMEM)
+    dma = pltpu.SemaphoreType.DMA
+    return pl.pallas_call(
+        functools.partial(output_kernel, count, row_count, inner_width),
+        out_shape=[
+            jax.ShapeDtypeStruct((tokens, depth), BF16),
+            jax.ShapeDtypeStruct(sent.shape, BF16),
+        ],
+        in_specs=[vmem] * 5,
+        out_specs=[vmem] * 2,
+        scratch_shapes=[
+            pltpu.VMEM((row_count, rows, inner), BF16),
+            pltpu.VMEM((count, tokens, depth + LANES), BF16),
+            pltpu.VMEM((count, tokens, depth + LANES), BF16),
+            pltpu.VMEM(sent.shape, BF16),
+            dma((chips,)),
+            dma((chips,)),
+            dma((chips,)),
+            dma((chips,)),
+            dma((count,)),
+            dma((count,)),
+            dma((count,)),
+            dma((count,)),
+        ],
+        compiler_params=pltpu.CompilerParams(
+            collective_id=2 * layer + 1, has_side_effects=True, vmem_limit_bytes=VMEM_LIMIT
+        ),
+        cost_estimate=SMALL,
+    )(gated, gain, weight, hidden, sent)
 
 
 def rotate(array, offset, count):
@@ -341,6 +615,7 @@
     mine = slot_requests[:SEND_CAP]
 
     picked = pick_states(slot_requests, state_cache, col_count)
+    hidden, picked = lax.optimization_barrier((hidden_states, picked))
     starts = [picked[0]] + [
         rotate(picked[offset], offset, col_count) for offset in range(1, col_count)
     ]
@@ -348,52 +623,37 @@
     head_rows = jnp.pad(
         jnp.stack([step_bias, decay_log, skip_gain], axis=1), ((0, 0), (0, 5), (0, 0))
     )
-    hidden = hidden_states
     states = None
     weight_layers = []
     b_layers = []
     for layer in range(layers):
-        tokens = lax.all_gather(hidden, "col", axis=0, tiled=True).astype(F32)
-        scaled = (tokens * input_gain[layer]).astype(BF16)
-        square = jnp.sum(tokens * tokens, axis=1, keepdims=True)
-        weight = inner_weight[layer].reshape(row_width, 2 * inner)
-        partial = jnp.concatenate(
+        weight = jnp.concatenate(
             [
-                jnp.dot(scaled, weight, preferred_element_type=F32),
-                jnp.dot(scaled, proj_weight[layer], preferred_element_type=F32),
-                jnp.dot(scaled, step_weight[layer], preferred_element_type=F32),
-                square,
-                jnp.zeros((tokens.shape[0], LANES - heads - 1), F32),
+                inner_weight[layer].reshape(row_width, 2 * inner),
+                proj_weight[layer],
+                step_weight[layer],
+                jnp.zeros((row_width, LANES - heads), BF16),
             ],
             axis=1,
         )
-        proj = lax.psum_scatter(partial, "row", scatter_dimension=0, tiled=True)
+        proj = project(
+            layer, col_count, row_count, heads, hidden, input_gain[layer : layer + 1], weight
+        )
         states, gated, sent, b_half = scan_layer(
             layer, model_width, col_count, slots, accepted, live, proj, inner_cache, proj_cache,
             inner_kernel, proj_kernel, head_rows, state_cache, states,
         )
-        weight_layers.append(sent)
         b_layers.append(b_half)
-        gathered = lax.all_gather(gated, "row", axis=0, tiled=True).astype(F32)
-        gate_square = jnp.sum(gathered * gathered, axis=1, keepdims=True)
-        partial_out = jnp.dot(
-            (gathered * norm_gain[layer]).astype(BF16),
-            out_weight[layer],
-            preferred_element_type=F32,
-        )
-        message = jnp.concatenate(
-            [partial_out, jnp.broadcast_to(gate_square, (gathered.shape[0], LANES))], axis=1
-        ).astype(BF16)
-        total = lax.psum_scatter(message, "col", scatter_dimension=0, tiled=True).astype(F32)
-        factor = lax.rsqrt(total[:, row_width : row_width + 1] / inner_width + EPSILON)
-        hidden = (hidden.astype(F32) + total[:, :row_width] * factor).astype(BF16)
-
-    sent = jnp.stack(weight_layers).reshape(layers, col_count, SEND_CAP, S, inner + LANES)
-    received = [sent[:, 0]] + [
-        rotate(sent[:, offset], offset, col_count) for offset in range(1, col_count)
-    ]
+        if layer == layers - 1:
+            gated, starts = lax.optimization_barrier((gated, starts))
+        hidden, received = output(
+            layer, col_count, row_count, inner_width, gated, norm_gain[layer : layer + 1],
+            out_weight[layer], hidden,
+            sent.reshape(col_count, SEND_CAP, S, inner + LANES),
+        )
+        weight_layers.append(received)
     owned = owned_states(
-        mine, jnp.stack(received, axis=1), jnp.stack(b_layers), starts, layers, heads, size, state
+        mine, jnp.stack(weight_layers), jnp.stack(b_layers), starts, layers, heads, size, state
     )
     return (hidden, states, owned)
 

time: 426 us -> 268 us (0.63)
  waiting for transfers between devices: 199 us -> 0.02 us
  Pallas kernels: 48.5 us -> 224 us
  blocking collectives: 78.2 us -> 0 us
  starting transfers between devices: 43.6 us -> 19.5 us
  local copies, waits for them, and re-layouts: 32.5 us -> 16.8 us
  between operations: 14.3 us -> 0.97 us
  matrix products: 6.29 us -> 0 us
    pallas_call x0 -> x4, Pallas kernels: none -> 174 us  [the longest x2 106 us: project(): pl.pallas_call(functools.partial(project_kernel, count, row_count, heads)...]
    unnamed x6 -> x0, waiting for transfers between devices: 84.5 us -> none
    all_gather x4 -> x0, blocking collectives: 78.2 us -> none  [the longest x2 64.7 us: local(): tokens = lax.all_gather(hidden, 'col', axis=0, tiled=True).astype(F32)]
    reduce_scatter x2 -> x0, waiting for transfers between devices: 63 us -> none  [local(): proj = lax.psum_scatter(partial, 'row', scatter_dimension=0, tiled=True)]
    ppermute x14 -> x7, waiting for transfers between devices: 51.1 us -> 0.02 us  [rotate(): lax.ppermute(array, 'col', [(c, (c + offset) % count) for c in range(coun...]
    ppermute x14 -> x7, starting transfers between devices: 43.5 us -> 19.5 us  [rotate(): lax.ppermute(array, 'col', [(c, (c + offset) % count) for c in range(coun...]
    unnamed x78 -> x47, local copies, waits for them, and re-layouts: 21.6 us -> 8.41 us
    dot_general x8 -> x0, matrix products: 6.29 us -> none  [the longest x2 2.65 us: local(): jnp.dot(scaled, weight, preferred_element_type=F32)]
  transfers between devices with their start and end apart: 18 -> 7, of which waited for: 8 -> 0; matrix products, arithmetic and copies ran while one was open for 2% -> 5% of each run, Pallas kernels for 7% -> 70%
where the time goes in v2:
time: 268 us; the launch traced here: 264 us
  Pallas kernels  224 us (84%)
  starting transfers between devices  19.5 us (7%)
  local copies, waits for them, and re-layouts  16.8 us (6%)
    pallas_call x2, Pallas kernels, project(): pl.pallas_call(functools.partial(project_kernel, count, row_count, heads)...  106 us
    pallas_call x2, Pallas kernels, output(): pl.pallas_call(functools.partial(output_kernel, count, row_count, inner_w...  67.8 us
    pallas_call x2, Pallas kernels, scan_layer(): pl.pallas_call(functools.partial(scan_kernel, model_width), grid_spec=plt...  39.3 us
    ppermute x7, starting transfers between devices, rotate(): lax.ppermute(array, 'col', [(c, (c + offset) % count) for c in range(coun...  19.5 us
    unnamed x47, local copies, waits for them, and re-layouts  8.41 us
    pallas_call x1, Pallas kernels, owned_states(): pl.pallas_call(functools.partial(owned_kernel, heads, size), grid_spec=pl...  7.03 us
  transfers between devices with their start and end apart: 7, of which 0 were waited for; matrix products, arithmetic and copies ran while one was open for 5% of the time, Pallas kernels for 70%

profile of v2, /device:TPU:0, one launch (start us, length us, event | category | flops | bytes accessed | tf_op | source)
XLA Modules:
  0.0 264.2 jit_solution(18149689245134358518)
XLA Ops:
  0.6 0.0 copy-start.18
  0.6 0.0 copy-start.15
  0.7 0.0 copy-start.14
  0.7 0.0 copy-start.13
  0.7 0.9 convert_reduce_fusion
  1.6 0.7 fusion.3.slots
  2.3 0.1 select_reduce_fusion.slots
  2.3 4.2 %shard_map.193 = (bf16[2,2,8,64,128]{4,3,2,1,0:T(8,128)(2,1)S(1)}, bf16[2,2,8,64,128]{4,3,2,1,0:T(8,128)(2,1)}, bf16[2,2,8,64,128]{4,3,2,1,0:T(8,128)(2,1)}, bf1...) custom-call(s32[16]{0:T(128)S(1)} %select_reduce_fusion.slots, ...), custom_call_target="tpu_custom_call" | custom-call | bytes 8388608 | tf_op jit(solution)/shard_map/pallas_call | solution.py:45
  6.5 0.8 copy-done.6
  7.3 0.8 copy-done.8
  8.1 2.9 %collective-permute-start = (bf16[2,2,8,64,128]{4,3,2,1,0:T(8,128)(2,1)}, bf16[2,2,8,64,128]{4,3,2,1,0:T(8,128)(2,1)}, u32[]{:S(2)}, u32[]{:S(2)}) collective-permute-start(bf16[2,2,8,64,128]{4,3,2,1,0:T(8,128)(2,1)} %get-tuple-element.56), channel_id=1, source_target_pairs={{0,1},{1,2},{2,3},{3,4},{4,5},{5,6},{6,7},{7,0},{8,9},{9,10},{10,1... | collective-permute-start | bytes 1572872 | tf_op jit(solution)/shard_map/ppermute | solution.py:566
  11.1 1.6 collective-permute-start.1
  12.7 2.6 collective-permute-start.2
  15.2 1.2 collective-permute-start.3
  16.4 2.6 collective-permute-start.4
  19.1 0.0 copy-done.18
  19.1 0.1 and_reduce_fusion
  19.2 0.0 copy-done.15
  19.2 0.0 copy-done.14
  19.2 0.0 copy-done.13
  19.3 0.8 copy.41
  20.1 0.8 copy.40
  20.9 2.7 %fusion.4 = (bf16[1,512,2,512]{3,2,1,0:T(2,128)(2,1)S(1)}, bf16[1,512,2,512]{3,2,1,0:T(2,128)(2,1)S(1)}) fusion(bf16[2,512,2,512]{3,2,1,0:T(2,128)(2,1)} %param.20), kind=kLoop, calls=%fused_computation.23 | loop fusion | bytes 4194304 | tf_op jit(solution)/shard_map/slice | solution.py:632
  23.6 0.2 copy.43
  23.9 0.0 copy-start.16
  23.9 1.2 copy.42
  25.1 0.0 copy-done.12
  25.1 0.7 slice_bitcast_fusion.2
  25.9 0.0 copy-start.10
  25.9 2.3 concatenate.7.weight_ref
  28.2 0.0 copy-done.10
  28.2 2.5 concatenate.6.weight_ref
  30.7 0.0 copy-done.16
  30.7 0.0 copy-start.17
  30.8 0.0 copy-start.2
  30.8 0.8 copy-done.2
  31.6 78.8 %shard_map.194.proj_ref = f32[128,1408]{1,0:T(8,128)S(1)} custom-call(bf16[64,512]{1,0:T(8,128)(2,1)S(1)} %copy-done.2, f32[1,512]{1,0:T(1,128)S(1)} %get-tuple-element.90.gain_ref, bf16[512,1408]{1,0:T(8,128)(2,1)S(1)} %concatenate.6.weight_ref), custom_call_target="tpu_custom_call" | custom-call | flops 1000000 | bytes 1000000 | tf_op jit(solution)/shard_map/pallas_call | solution.py:415
  110.4 0.0 copy-done.19
  110.4 0.7 select_maximum_fusion.head_ref
  111.1 0.0 copy-done.3
  111.1 0.0 copy-done.4
  111.1 0.0 copy-done.5
  111.1 0.0 copy-start
  111.2 2.2 copy-done
  113.3 19.7 %shard_map.195 = (bf16[2,8,16,8,64,128]{5,4,3,2,1,0:T(8,128)(2,1)}, bf16[128,512]{1,0:T(8,128)(2,1)S(1)}, bf16[16,16,640]{2,1,0:T(8,128)(2,1)S(1)}, bf16[8,16,128]{2,1,0:T(8,128)(2,1)S(1)}) custom-call(s32[8]{0:T(128)S(1)} %fusion.3.slots, s32[8]{0:T(128)S(1)} %copy-done.5, s32[8]{0:T(128)S(1)} %convert_element_type.9.live, ...), custom_call_target="tpu_custom_call" | custom-call | flops 1000000 | bytes 1000000 | tf_op jit(solution)/shard_map/pallas_call | solution.py:209
  133.0 0.0 collective-permute-done.rest_1_
  133.0 7.6 %collective-permute-start.5 = (bf16[2,2,8,64,128]{4,3,2,1,0:T(8,128)(2,1)S(1)}, bf16[2,2,8,64,128]{4,3,2,1,0:T(8,128)(2,1)S(1)}, u32[]{:S(2)}, u32[]{:S(2)}) collective-permute-start(bf16[2,2,8,64,128]{4,3,2,1,0:T(8,128)(2,1)S(1)} %copy-done.9), channel_id=1, source_target_pairs={{0,6},{1,7},{2,0},{3,1},{4,2},{5,3},{6,4},{7,5},{8,14},{9,15},{10,... | collective-permute-start | bytes 1572872 | tf_op jit(solution)/shard_map/ppermute | solution.py:566
  140.6 0.0 collective-permute-done.1.rest_2_
  140.6 0.9 collective-permute-start.6
  141.6 0.0 copy-done.17
  141.6 0.1 slice_bitcast_fusion
  141.6 39.1 %shard_map.196 = (bf16[64,512]{1,0:T(8,128)(2,1)S(1)}, bf16[8,2,16,640]{3,2,1,0:T(8,128)(2,1)S(1)}) custom-call(bf16[128,512]{1,0:T(8,128)(2,1)S(1)} %get-tuple-element.50.gated_ref, f32[1,512]{1,0:T(1,128)S(1)} %get-tuple-element.88.gain_ref, bf16[512,512]{1,0:T(8,128)(2,1)S(1)} %get-tuple-element.82.weight_ref, bf16[64,512]{1,0:T(8,128)(2,1)S(1)} %copy-done.2, ...), custom_call_target="tpu_custom_call" | custom-call | flops 1000000 | bytes 1000000 | tf_op jit(solution)/shard_map/pallas_call | solution.py:536
  180.7 27.2 %shard_map.197.proj_ref = f32[128,1408]{1,0:T(8,128)S(1)} custom-call(bf16[64,512]{1,0:T(8,128)(2,1)S(1)} %get-tuple-element.52.hidden_ref, f32[1,512]{1,0:T(1,128)S(1)} %get-tuple-element.89.gain_ref, bf16[512,1408]{1,0:T(8,128)(2,1)S(1)} %concatenate.7.weight_ref), custom_call_target="tpu_custom_call" | custom-call | flops 1000000 | bytes 1000000 | tf_op jit(solution)/shard_map/pallas_call | solution.py:415
  208.0 0.0 copy-done.1
  208.0 19.7 %shard_map.198 = (bf16[2,8,16,8,64,128]{5,4,3,2,1,0:T(8,128)(2,1)}, bf16[128,512]{1,0:T(8,128)(2,1)S(1)}, bf16[16,16,640]{2,1,0:T(8,128)(2,1)S(1)}, bf16[8,16,128]{2,1,0:T(8,128)(2,1)S(1)}) custom-call(s32[8]{0:T(128)S(1)} %fusion.3.slots, s32[8]{0:T(128)S(1)} %copy-done.5, s32[8]{0:T(128)S(1)} %convert_element_type.9.live, ...), custom_call_target="tpu_custom_call", output_to_operand_aliasing={{0}: (10, {})} | custom-call | flops 1000000 | bytes 1000000 | tf_op jit(solution)/shard_map/pallas_call | solution.py:209
  227.7 0.0 collective-permute-done.2.rest_3_
  227.7 0.0 collective-permute-done.3.rest_4_
  227.7 0.0 collective-permute-done.4.rest_5_
  227.7 0.0 collective-permute-done.5.rest_6_
  227.7 0.0 collective-permute-done.6.rest_7_
  227.7 28.7 %shard_map.199 = (bf16[64,512]{1,0:T(8,128)(2,1)S(1)}, bf16[8,2,16,640]{3,2,1,0:T(8,128)(2,1)S(1)}) custom-call(bf16[128,512]{1,0:T(8,128)(2,1)S(1)} %get-tuple-element.63.gated_ref, f32[1,512]{1,0:T(1,128)S(1)} %get-tuple-element.87.gain_ref, bf16[512,512]{1,0:T(8,128)(2,1)S(1)} %get-tuple-element.81.weight_ref, ...), custom_call_target="tpu_custom_call" | custom-call | flops 1000000 | bytes 1000000 | tf_op jit(solution)/shard_map/pallas_call | solution.py:536
  256.4 0.1 pad_maximum_fusion.weights_ref
  256.5 7.0 %shard_map.200 = bf16[1,1,2,2,64,64,128]{6,5,4,3,2,1,0:T(8,128)(2,1)} custom-call(s32[2]{0:T(128)S(1)} %bitcast.42, bf16[2,8,2,16,640]{4,3,2,1,0:T(8,128)(2,1)S(1)} %pad_maximum_fusion.weights_ref, bf16[2,8,16,128]{3,2,1,0:T(8,128)(2,1)S(1)} %pad_maximum_fusion.1.b_ref, bf16[2,2,8,64,128]{4,3,2,1,0:T(8,128)(2,1)S(1)} %get-tuple-element.71.rest_0_, ...), custom_call_target="tpu_custom_call" | custom-call | tf_op jit(solution)/shard_map/pallas_call | solution.py:267
  263.5 0.6 copy.46
  (24 shorter events, 0.1 us)
Async XLA Ops:
  0.6 18.4 %copy-start.18 = (s32[4,2]{0,1:T(2,128)S(1)}, s32[4,2]{0,1:T(2,128)}, u32[]{:S(2)}) copy-start(s32[4,2]{0,1:T(2,128)} %param.35) | copy-start | bytes 100
  0.6 18.5 %copy-start.15 = (bf16[2,512,8]{1,2,0:T(8,128)(2,1)S(1)}, bf16[2,512,8]{1,2,0:T(8,128)(2,1)}, u32[]{:S(2)}) copy-start(bf16[2,512,8]{1,2,0:T(8,128)(2,1)} %param.22) | copy-start | bytes 49156
  0.7 18.5 %copy-start.14 = (bf16[2,8,3,256]{3,1,2,0:T(8,128)(2,1)S(1)}, bf16[2,8,3,256]{3,1,2,0:T(8,128)(2,1)}, u32[]{:S(2)}) copy-start(bf16[2,8,3,256]{3,1,2,0:T(8,128)(2,1)} %param.31) | copy-start | bytes 73732
  0.7 18.6 %copy-start.13 = (bf16[2,8,3,512]{3,1,2,0:T(8,128)(2,1)S(1)}, bf16[2,8,3,512]{3,1,2,0:T(8,128)(2,1)}, u32[]{:S(2)}) copy-start(bf16[2,8,3,512]{3,1,2,0:T(8,128)(2,1)} %param.30) | copy-start | bytes 147460
  6.5 0.8 copy-start.6
  7.3 0.8 copy-start.8
  8.1 124.9 %collective-permute-start = (bf16[2,2,8,64,128]{4,3,2,1,0:T(8,128)(2,1)}, bf16[2,2,8,64,128]{4,3,2,1,0:T(8,128)(2,1)}, u32[]{:S(2)}, u32[]{:S(2)}) collective-permute-start(bf16[2,2,8,64,128]{4,3,2,1,0:T(8,128)(2,1)} %get-tuple-element.56), channel_id=1, source_target_pairs={{0,1},{1,2},{2,3},{3,4},{4,5},{5,6},{6,7},{7,0},{8,9},{9,10},{10,1... | collective-permute-start | bytes 1572872 | tf_op jit(solution)/shard_map/ppermute | solution.py:566
  11.1 129.5 %collective-permute-start.1 = (bf16[2,2,8,64,128]{4,3,2,1,0:T(8,128)(2,1)}, bf16[2,2,8,64,128]{4,3,2,1,0:T(8,128)(2,1)}, u32[]{:S(2)}, u32[]{:S(2)}) collective-permute-start(bf16[2,2,8,64,128]{4,3,2,1,0:T(8,128)(2,1)} %get-tuple-element.57), channel_id=1, source_target_pairs={{0,2},{1,3},{2,4},{3,5},{4,6},{5,7},{6,0},{7,1},{8,10},{9,11},{10,... | collective-permute-start | bytes 1572872 | tf_op jit(solution)/shard_map/ppermute | solution.py:566
  12.7 215.0 %collective-permute-start.2 = (bf16[2,2,8,64,128]{4,3,2,1,0:T(8,128)(2,1)}, bf16[2,2,8,64,128]{4,3,2,1,0:T(8,128)(2,1)}, u32[]{:S(2)}, u32[]{:S(2)}) collective-permute-start(bf16[2,2,8,64,128]{4,3,2,1,0:T(8,128)(2,1)} %get-tuple-element.58), channel_id=1, source_target_pairs={{0,3},{1,4},{2,5},{3,6},{4,7},{5,0},{6,1},{7,2},{8,11},{9,12},{10,... | collective-permute-start | bytes 1572872 | tf_op jit(solution)/shard_map/ppermute | solution.py:566
  15.2 212.5 %collective-permute-start.3 = (bf16[2,2,8,64,128]{4,3,2,1,0:T(8,128)(2,1)}, bf16[2,2,8,64,128]{4,3,2,1,0:T(8,128)(2,1)}, u32[]{:S(2)}, u32[]{:S(2)}) collective-permute-start(bf16[2,2,8,64,128]{4,3,2,1,0:T(8,128)(2,1)} %get-tuple-element.59), channel_id=1, source_target_pairs={{0,4},{1,5},{2,6},{3,7},{4,0},{5,1},{6,2},{7,3},{8,12},{9,13},{10,... | collective-permute-start | bytes 1572872 | tf_op jit(solution)/shard_map/ppermute | solution.py:566
  16.4 211.2 %collective-permute-start.4 = (bf16[2,2,8,64,128]{4,3,2,1,0:T(8,128)(2,1)}, bf16[2,2,8,64,128]{4,3,2,1,0:T(8,128)(2,1)}, u32[]{:S(2)}, u32[]{:S(2)}) collective-permute-start(bf16[2,2,8,64,128]{4,3,2,1,0:T(8,128)(2,1)} %get-tuple-element.60), channel_id=1, source_target_pairs={{0,5},{1,6},{2,7},{3,0},{4,1},{5,2},{6,3},{7,4},{8,13},{9,14},{10,... | collective-permute-start | bytes 1572872 | tf_op jit(solution)/shard_map/ppermute | solution.py:566
  20.9 4.2 %copy-start.12 = (bf16[2,512,256]{2,1,0:T(8,128)(2,1)S(1)}, bf16[2,512,256]{2,1,0:T(8,128)(2,1)}, u32[]{:S(2)}) copy-start(bf16[2,512,256]{2,1,0:T(8,128)(2,1)} %param.21) | copy-start | bytes 1572868
  23.9 6.9 %copy-start.16 = (f32[2,512]{1,0:T(2,128)S(1)}, f32[2,512]{1,0:T(2,128)}, u32[]{:S(2)}) copy-start(f32[2,512]{1,0:T(2,128)} %param.19) | copy-start | bytes 12292
  25.8 84.6 %copy-start.19 = (f32[2,8]{1,0:T(2,128)S(1)}, f32[2,8]{1,0:T(2,128)}, u32[]{:S(2)}) copy-start(f32[2,8]{1,0:T(2,128)} %param.27) | copy-start | bytes 196
  25.8 85.3 %copy-start.3 = (f32[2,4,512]{2,1,0:T(4,128)S(1)}, f32[2,4,512]{2,1,0:T(4,128)}, u32[]{:S(2)}) copy-start(f32[2,4,512]{2,1,0:T(4,128)} %inner_kernel.3) | copy-start | bytes 49156
  25.8 85.3 %copy-start.4 = (f32[2,4,256]{2,1,0:T(4,128)S(1)}, f32[2,4,256]{2,1,0:T(4,128)}, u32[]{:S(2)}) copy-start(f32[2,4,256]{2,1,0:T(4,128)} %proj_kernel.3) | copy-start | bytes 24580
  25.8 85.3 %copy-start.5 = (s32[8]{0:T(128)S(1)}, s32[8]{0:T(128)}, u32[]{:S(2)}) copy-start(s32[8]{0:T(128)} %accepted.3) | copy-start | bytes 100
  25.9 2.3 copy-start.10
  30.7 110.8 %copy-start.17 = (f32[2,512]{1,0:T(2,128)S(1)}, f32[2,512]{1,0:T(2,128)}, u32[]{:S(2)}) copy-start(f32[2,512]{1,0:T(2,128)} %param.28) | copy-start | bytes 12292
  30.8 0.8 copy-start.2
  31.6 101.4 %copy-start.9 = (bf16[2,2,8,64,128]{4,3,2,1,0:T(8,128)(2,1)S(1)}, bf16[2,2,8,64,128]{4,3,2,1,0:T(8,128)(2,1)}, u32[]{:S(2)}) copy-start(bf16[2,2,8,64,128]{4,3,2,1,0:T(8,128)(2,1)} %copy-done.8) | copy-start | bytes 1572868
  31.6 109.0 %copy-start.7 = (bf16[2,2,8,64,128]{4,3,2,1,0:T(8,128)(2,1)S(1)}, bf16[2,2,8,64,128]{4,3,2,1,0:T(8,128)(2,1)}, u32[]{:S(2)}) copy-start(bf16[2,2,8,64,128]{4,3,2,1,0:T(8,128)(2,1)} %copy-done.6) | copy-start | bytes 1572868
  31.6 110.0 %copy-start.11 = (bf16[2,512,512]{2,1,0:T(8,128)(2,1)S(1)}, bf16[2,512,512]{2,1,0:T(8,128)(2,1)}, u32[]{:S(2)}) copy-start(bf16[2,512,512]{2,1,0:T(8,128)(2,1)} %param.29) | copy-start | bytes 3145732
  111.1 2.2 copy-start
  113.3 94.6 %copy-start.1 = (f32[2,8,8,64,128]{4,3,2,1,0:T(8,128)S(1)}, f32[2,8,8,64,128]{4,3,2,1,0:T(8,128)}, u32[]{:S(2)}) copy-start(f32[2,8,8,64,128]{4,3,2,1,0:T(8,128)} %state_ref.5) | copy-start | bytes 12582916
  133.0 94.7 %collective-permute-start.5 = (bf16[2,2,8,64,128]{4,3,2,1,0:T(8,128)(2,1)S(1)}, bf16[2,2,8,64,128]{4,3,2,1,0:T(8,128)(2,1)S(1)}, u32[]{:S(2)}, u32[]{:S(2)}) collective-permute-start(bf16[2,2,8,64,128]{4,3,2,1,0:T(8,128)(2,1)S(1)} %copy-done.9), channel_id=1, source_target_pairs={{0,6},{1,7},{2,0},{3,1},{4,2},{5,3},{6,4},{7,5},{8,14},{9,15},{10,... | collective-permute-start | bytes 1572872 | tf_op jit(solution)/shard_map/ppermute | solution.py:566
  140.6 87.1 %collective-permute-start.6 = (bf16[2,2,8,64,128]{4,3,2,1,0:T(8,128)(2,1)S(1)}, bf16[2,2,8,64,128]{4,3,2,1,0:T(8,128)(2,1)S(1)}, u32[]{:S(2)}, u32[]{:S(2)}) collective-permute-start(bf16[2,2,8,64,128]{4,3,2,1,0:T(8,128)(2,1)S(1)} %copy-done.7), channel_id=1, source_target_pairs={{0,7},{1,0},{2,1},{3,2},{4,3},{5,4},{6,5},{7,6},{8,15},{9,8},{10,9... | collective-permute-start | bytes 1572872 | tf_op jit(solution)/shard_map/ppermute | solution.py:566

commit v3 on v2

--- a/solution.py
+++ b/solution.py
@@ -458,6 +458,13 @@
             )
         )
     state_copies = []
+    for offset in range(1, count):
+        state_copies.append(
+            push(
+                sent_ref.at[offset], taken.at[offset], state_send.at[offset],
+                state_recv.at[offset], {"col": lax.rem(column + offset, count)},
+            )
+        )
 
     def process(group, owner):
         value = group.astype(F32)
@@ -496,13 +503,6 @@
     for step in range(1, chips):
         relays[step - 1].wait_recv()
         process(groups[2 * step + 1], lax.rem(chip + step, chips) * 2 + 1 - core)
-    for offset in range(1, count):
-        state_copies.append(
-            push(
-                sent_ref.at[offset], taken.at[offset], state_send.at[offset],
-                state_recv.at[offset], {"col": lax.rem(column + offset, count)},
-            )
-        )
     received_ref[0] = sent_ref[0]
     total = outbox[column].astype(F32)
     for offset in range(1, count):
@@ -616,10 +616,28 @@
 
     picked = pick_states(slot_requests, state_cache, col_count)
     hidden, picked = lax.optimization_barrier((hidden_states, picked))
-    starts = [picked[0]] + [
-        rotate(picked[offset], offset, col_count) for offset in range(1, col_count)
-    ]
-
+    picked = list(picked)
+    starts = [picked[0]] + [None] * (col_count - 1)
+
+    def turn_of(offset):
+        if offset % 8 in (1, 7):
+            return 0
+        return 1 if offset % 8 in (2, 4, 6) else 2
+
+    def send_turn(turn, after):
+        offsets = [offset for offset in range(1, col_count) if turn_of(offset) == turn]
+        blocks = [picked[offset] for offset in offsets]
+        if after is not None:
+            after, blocks = lax.optimization_barrier((after, blocks))
+        for offset, block in zip(offsets, blocks):
+            starts[offset] = rotate(block, offset, col_count)
+        return after
+
+    send_turn(0, None)
+    early = [offset for offset in range(1, col_count) if turn_of(offset) == 0]
+    hidden, arrived = lax.optimization_barrier((hidden, [starts[offset] for offset in early]))
+    for offset, block in zip(early, arrived):
+        starts[offset] = block
     head_rows = jnp.pad(
         jnp.stack([step_bias, decay_log, skip_gain], axis=1), ((0, 0), (0, 5), (0, 0))
     )
@@ -639,13 +657,15 @@
         proj = project(
             layer, col_count, row_count, heads, hidden, input_gain[layer : layer + 1], weight
         )
+        if layer == 0:
+            proj = send_turn(1, proj)
+        if layer == layers - 1:
+            proj = send_turn(2, proj)
         states, gated, sent, b_half = scan_layer(
             layer, model_width, col_count, slots, accepted, live, proj, inner_cache, proj_cache,
             inner_kernel, proj_kernel, head_rows, state_cache, states,
         )
         b_layers.append(b_half)
-        if layer == layers - 1:
-            gated, starts = lax.optimization_barrier((gated, starts))
         hidden, received = output(
             layer, col_count, row_count, inner_width, gated, norm_gain[layer : layer + 1],
             out_weight[layer], hidden,

time: 268 us -> 227 us (0.85)
  Pallas kernels: 224 us -> 171 us
  waiting for transfers between devices: 0.02 us -> 5.42 us
  local copies, waits for them, and re-layouts: 16.8 us -> 21.8 us
    pallas_call x2, Pallas kernels: 106 us -> 47.3 us  [project(): pl.pallas_call(functools.partial(project_kernel, count, row_count, heads)...]
    pallas_call x2, Pallas kernels: 67.8 us -> 73.9 us  [output(): pl.pallas_call(functools.partial(output_kernel, count, row_count, inner_w...]
    ppermute x7, waiting for transfers between devices: 0.02 us -> 5.42 us  [rotate(): lax.ppermute(array, 'col', [(c, (c + offset) % count) for c in range(coun...]
    unnamed x47 -> x57, local copies, waits for them, and re-layouts: 8.41 us -> 10.5 us
  transfers between devices with their start and end apart: 7 -> 7, of which waited for: 0 -> 2; matrix products, arithmetic and copies ran while one was open for 5% -> 7% of each run, Pallas kernels for 70% -> 62%
where the time goes in v3:
time: 227 us; the launch traced here: 222 us
  Pallas kernels  171 us (75%)
  local copies, waits for them, and re-layouts  21.8 us (10%)
  starting transfers between devices  20.7 us (9%)
  waiting for transfers between devices  5.42 us (2%)
  other arithmetic  2.37 us (1%)
    pallas_call x2, Pallas kernels, output(): pl.pallas_call(functools.partial(output_kernel, count, row_count, inner_w...  73.9 us
    pallas_call x2, Pallas kernels, project(): pl.pallas_call(functools.partial(project_kernel, count, row_count, heads)...  47.3 us
    pallas_call x2, Pallas kernels, scan_layer(): pl.pallas_call(functools.partial(scan_kernel, model_width), grid_spec=plt...  39.4 us
    ppermute x7, starting transfers between devices, rotate(): lax.ppermute(array, 'col', [(c, (c + offset) % count) for c in range(coun...  20.7 us
    unnamed x57, local copies, waits for them, and re-layouts  10.5 us
    pallas_call x1, Pallas kernels, owned_states(): pl.pallas_call(functools.partial(owned_kernel, heads, size), grid_spec=pl...  6.71 us
    ppermute x7, waiting for transfers between devices, rotate(): lax.ppermute(array, 'col', [(c, (c + offset) % count) for c in range(coun...  5.42 us
    concatenate x2, local copies, waits for them, and re-layouts, local(): jnp.concatenate([inner_weight[layer].reshape(row_width, 2 * inner), proj_...  4.82 us
  transfers between devices with their start and end apart: 7, of which 2 were waited for; matrix products, arithmetic and copies ran while one was open for 7% of the time, Pallas kernels for 62%

profile of v3, /device:TPU:0, one launch (start us, length us, event | category | flops | bytes accessed | tf_op | source)
XLA Modules:
  0.0 222.4 jit_solution(1722772874028711969)
XLA Ops:
  0.6 0.0 copy-start.21
  0.6 0.0 copy-start.20
  0.7 0.0 copy-start.19
  0.7 0.9 convert_reduce_fusion
  1.6 0.7 fusion.3.slots
  2.3 0.1 select_reduce_fusion.slots
  2.4 0.0 copy-start.24
  2.4 0.0 copy-start.18
  2.4 0.0 copy-start.17
  2.4 3.8 %shard_map.193 = (bf16[2,2,8,64,128]{4,3,2,1,0:T(8,128)(2,1)S(1)}, bf16[2,2,8,64,128]{4,3,2,1,0:T(8,128)(2,1)}, bf16[2,2,8,64,128]{4,3,2,1,0:T(8,128)(2,1)S(1)},...) custom-call(s32[16]{0:T(128)S(1)} %select_reduce_fusion.slots, ...), custom_call_target="tpu_custom_call" | custom-call | bytes 8388608 | tf_op jit(solution)/shard_map/pallas_call | solution.py:45
  6.2 0.8 copy-done.8
  7.0 0.8 copy-done.10
  7.8 0.8 copy-done.12
  8.6 0.8 copy-done.13
  9.3 0.8 copy-done.14
  10.2 2.9 %collective-permute-start = (bf16[2,2,8,64,128]{4,3,2,1,0:T(8,128)(2,1)}, bf16[2,2,8,64,128]{4,3,2,1,0:T(8,128)(2,1)}, u32[]{:S(2)}, u32[]{:S(2)}) collective-permute-start(bf16[2,2,8,64,128]{4,3,2,1,0:T(8,128)(2,1)} %get-tuple-element.51), channel_id=1, source_target_pairs={{0,1},{1,2},{2,3},{3,4},{4,5},{5,6},{6,7},{7,0},{8,9},{9,10},{10,1... | collective-permute-start | bytes 1572872 | tf_op jit(solution)/shard_map/ppermute | solution.py:566
  13.1 3.0 %collective-permute-start.1 = (bf16[2,2,8,64,128]{4,3,2,1,0:T(8,128)(2,1)}, bf16[2,2,8,64,128]{4,3,2,1,0:T(8,128)(2,1)}, u32[]{:S(2)}, u32[]{:S(2)}) collective-permute-start(bf16[2,2,8,64,128]{4,3,2,1,0:T(8,128)(2,1)} %get-tuple-element.52), channel_id=1, source_target_pairs={{0,7},{1,0},{2,1},{3,2},{4,3},{5,4},{6,5},{7,6},{8,15},{9,8},{10,9... | collective-permute-start | bytes 1572872 | tf_op jit(solution)/shard_map/ppermute | solution.py:566
  16.2 0.7 slice_bitcast_fusion.2
  16.9 3.5 %fusion.4 = (bf16[1,512,2,512]{3,2,1,0:T(2,128)(2,1)}, bf16[1,512,2,512]{3,2,1,0:T(2,128)(2,1)S(1)}) fusion(bf16[2,512,2,512]{3,2,1,0:T(2,128)(2,1)} %param.20), kind=kLoop, calls=%fused_computation.23 | loop fusion | bytes 4194304 | tf_op jit(solution)/shard_map/slice | solution.py:650
  20.4 0.0 copy-done.5
  20.4 0.1 and_reduce_fusion
  20.5 0.0 copy-done.23
  20.5 0.0 copy-done.24
  20.5 0.5 convert_element_type.9.live
  21.0 0.0 copy-done.18
  21.1 0.0 copy-done.17
  21.1 0.8 copy.41
  21.9 0.8 copy.40
  22.7 1.5 copy.43
  24.1 1.2 copy.42
  25.4 2.3 %concatenate.7.weight_ref = bf16[512,1408]{1,0:T(8,128)(2,1)S(1)} concatenate(bf16[512,1024]{1,0:T(8,128)(2,1)S(1)} %bitcast.44, bf16[512,256]{1,0:T(8,128)(2,1)S(1)} %get-tuple-element.85, bf16[512,8]{1,0:T(8,128)(2,1)} %bitcast.48, bf16[512,120]{1,0:T(8,128)(2,1)S(1)} %broadcast.25), dimensions={1} | concatenate | bytes 2883584 | tf_op jit(solution)/shard_map/concatenate | solution.py:648
  27.7 0.0 copy-start.2
  27.8 0.0 copy-start.3
  27.8 0.0 copy-start.4
  27.8 2.5 %concatenate.6.weight_ref = bf16[512,1408]{1,0:T(8,128)(2,1)S(1)} concatenate(bf16[512,1024]{1,0:T(8,128)(2,1)} %bitcast.43, bf16[512,256]{1,0:T(8,128)(2,1)} %get-tuple-element.86, bf16[512,8]{1,0:T(8,128)(2,1)} %bitcast.47, bf16[512,120]{1,0:T(8,128)(2,1)} %copy-done.15), dimensions={1} | concatenate | bytes 2883584 | tf_op jit(solution)/shard_map/concatenate | solution.py:648
  30.3 0.0 copy-start
  30.3 0.9 fusion.6
  31.2 1.5 slice_bitcast_fusion
  32.6 3.2 %collective-permute-done.rest_1_ = bf16[2,2,8,64,128]{4,3,2,1,0:T(8,128)(2,1)} collective-permute-done((bf16[2,2,8,64,128]{4,3,2,1,0:T(8,128)(2,1)}, bf16[2,2,8,64,128]{4,3,2,1,0:T(8,128)(2,1)}, u32[]{:S(2)}, u32[]{:S(2)}) %collective-permute-start) | collective-permute-done | bytes 524320 | tf_op jit(solution)/shard_map/ppermute | solution.py:566
  35.8 2.2 collective-permute-done.1.rest_7_
  38.0 0.8 copy-done.1
  38.9 22.1 %shard_map.194.proj_ref = f32[128,1408]{1,0:T(8,128)S(1)} custom-call(bf16[64,512]{1,0:T(8,128)(2,1)S(1)} %copy-done.1, f32[1,512]{1,0:T(1,128)S(1)} %get-tuple-element.92.gain_ref, bf16[512,1408]{1,0:T(8,128)(2,1)S(1)} %concatenate.6.weight_ref), custom_call_target="tpu_custom_call" | custom-call | flops 1000000 | bytes 1000000 | tf_op jit(solution)/shard_map/pallas_call | solution.py:415
  60.9 3.4 %collective-permute-start.2 = (bf16[2,2,8,64,128]{4,3,2,1,0:T(8,128)(2,1)}, bf16[2,2,8,64,128]{4,3,2,1,0:T(8,128)(2,1)S(1)}, u32[]{:S(2)}, u32[]{:S(2)}) collective-permute-start(bf16[2,2,8,64,128]{4,3,2,1,0:T(8,128)(2,1)} %copy-done.14), channel_id=1, source_target_pairs={{0,2},{1,3},{2,4},{3,5},{4,6},{5,7},{6,0},{7,1},{8,10},{9,11},{10,... | collective-permute-start | bytes 1572872 | tf_op jit(solution)/shard_map/ppermute | solution.py:566
  64.4 5.5 %collective-permute-start.4 = (bf16[2,2,8,64,128]{4,3,2,1,0:T(8,128)(2,1)}, bf16[2,2,8,64,128]{4,3,2,1,0:T(8,128)(2,1)S(1)}, u32[]{:S(2)}, u32[]{:S(2)}) collective-permute-start(bf16[2,2,8,64,128]{4,3,2,1,0:T(8,128)(2,1)} %copy-done.13), channel_id=1, source_target_pairs={{0,4},{1,5},{2,6},{3,7},{4,0},{5,1},{6,2},{7,3},{8,12},{9,13},{10,... | collective-permute-start | bytes 1572872 | tf_op jit(solution)/shard_map/ppermute | solution.py:566
  69.9 0.0 collective-permute-start.6
  69.9 0.0 copy-start.7
  69.9 0.6 copy-done.7
  70.6 19.7 %shard_map.195 = (bf16[2,8,16,8,64,128]{5,4,3,2,1,0:T(8,128)(2,1)}, bf16[128,512]{1,0:T(8,128)(2,1)S(1)}, bf16[16,16,640]{2,1,0:T(8,128)(2,1)S(1)}, bf16[8,16,128]{2,1,0:T(8,128)(2,1)S(1)}) custom-call(s32[8]{0:T(128)S(1)} %fusion.3.slots, s32[8]{0:T(128)S(1)} %copy-done.4, s32[8]{0:T(128)S(1)} %copy-done.7, f32[128,1408]{1,0:T(8,128)S(1)} %shard_map.194.proj_ref, ...), custom_call_target="tpu_custom_call" | custom-call | flops 1000000 | bytes 1000000 | tf_op jit(solution)/shard_map/pallas_call | solution.py:209
  90.3 42.4 %shard_map.196 = (bf16[64,512]{1,0:T(8,128)(2,1)S(1)}, bf16[8,2,16,640]{3,2,1,0:T(8,128)(2,1)S(1)}) custom-call(bf16[128,512]{1,0:T(8,128)(2,1)S(1)} %get-tuple-element.58.gated_ref, f32[1,512]{1,0:T(1,128)S(1)} %get-tuple-element.90.gain_ref, bf16[512,512]{1,0:T(8,128)(2,1)S(1)} %get-tuple-element.84.weight_ref, bf16[64,512]{1,0:T(8,128)(2,1)S(1)} %copy-done.1, ...), custom_call_target="tpu_custom_call" | custom-call | flops 1000000 | bytes 1000000 | tf_op jit(solution)/shard_map/pallas_call | solution.py:536
  132.7 25.2 %shard_map.197.proj_ref = f32[128,1408]{1,0:T(8,128)S(1)} custom-call(bf16[64,512]{1,0:T(8,128)(2,1)S(1)} %get-tuple-element.60.hidden_ref, f32[1,512]{1,0:T(1,128)S(1)} %get-tuple-element.91.gain_ref, bf16[512,1408]{1,0:T(8,128)(2,1)S(1)} %concatenate.7.weight_ref), custom_call_target="tpu_custom_call" | custom-call | flops 1000000 | bytes 1000000 | tf_op jit(solution)/shard_map/pallas_call | solution.py:415
  157.9 0.0 copy-done.11
  157.9 5.8 %collective-permute-start.3 = (bf16[2,2,8,64,128]{4,3,2,1,0:T(8,128)(2,1)S(1)}, bf16[2,2,8,64,128]{4,3,2,1,0:T(8,128)(2,1)S(1)}, u32[]{:S(2)}, u32[]{:S(2)}) collective-permute-start(bf16[2,2,8,64,128]{4,3,2,1,0:T(8,128)(2,1)S(1)} %copy-done.11), channel_id=1, source_target_pairs={{0,3},{1,4},{2,5},{3,6},{4,7},{5,0},{6,1},{7,2},{8,11},{9,12},{10,... | collective-permute-start | bytes 1572872 | tf_op jit(solution)/shard_map/ppermute | solution.py:566
  163.7 0.0 copy-done.9
  163.7 0.0 collective-permute-start.5
  163.7 19.7 %shard_map.198 = (bf16[2,8,16,8,64,128]{5,4,3,2,1,0:T(8,128)(2,1)}, bf16[128,512]{1,0:T(8,128)(2,1)S(1)}, bf16[16,16,640]{2,1,0:T(8,128)(2,1)S(1)}, bf16[8,16,128]{2,1,0:T(8,128)(2,1)S(1)}) custom-call(s32[8]{0:T(128)S(1)} %fusion.3.slots, s32[8]{0:T(128)S(1)} %copy-done.4, s32[8]{0:T(128)S(1)} %copy-done.7, ...), custom_call_target="tpu_custom_call", output_to_operand_aliasing={{0}: (10, {})} | custom-call | flops 1000000 | bytes 1000000 | tf_op jit(solution)/shard_map/pallas_call | solution.py:209
  183.4 31.5 %shard_map.199 = (bf16[64,512]{1,0:T(8,128)(2,1)S(1)}, bf16[8,2,16,640]{3,2,1,0:T(8,128)(2,1)S(1)}) custom-call(bf16[128,512]{1,0:T(8,128)(2,1)S(1)} %get-tuple-element.65.gated_ref, f32[1,512]{1,0:T(1,128)S(1)} %get-tuple-element.89.gain_ref, bf16[512,512]{1,0:T(8,128)(2,1)S(1)} %get-tuple-element.83.weight_ref, ...), custom_call_target="tpu_custom_call" | custom-call | flops 1000000 | bytes 1000000 | tf_op jit(solution)/shard_map/pallas_call | solution.py:536
  214.9 0.1 pad_maximum_fusion.weights_ref
  215.0 0.0 collective-permute-done.2.rest_2_
  215.0 0.0 collective-permute-done.4.rest_4_
  215.0 0.0 collective-permute-done.6.rest_6_
  215.0 0.0 collective-permute-done.3.rest_3_
  215.0 0.0 collective-permute-done.5.rest_5_
  215.1 6.7 %shard_map.200 = bf16[1,1,2,2,64,64,128]{6,5,4,3,2,1,0:T(8,128)(2,1)} custom-call(s32[2]{0:T(128)S(1)} %bitcast.42, bf16[2,8,2,16,640]{4,3,2,1,0:T(8,128)(2,1)S(1)} %pad_maximum_fusion.weights_ref, bf16[2,8,16,128]{3,2,1,0:T(8,128)(2,1)S(1)} %pad_maximum_fusion.1.b_ref, bf16[2,2,8,64,128]{4,3,2,1,0:T(8,128)(2,1)S(1)} %get-tuple-element.73.rest_0_, ...), custom_call_target="tpu_custom_call" | custom-call | tf_op jit(solution)/shard_map/pallas_call | solution.py:267
  221.8 0.6 copy.46
  (34 shorter events, 0.2 us)
Async XLA Ops:
  0.6 15.5 %copy-start.21 = (s32[4,2]{0,1:T(2,128)S(1)}, s32[4,2]{0,1:T(2,128)}, u32[]{:S(2)}) copy-start(s32[4,2]{0,1:T(2,128)} %param.35) | copy-start | bytes 100
  0.6 15.5 %copy-start.20 = (f32[2,512]{1,0:T(2,128)S(1)}, f32[2,512]{1,0:T(2,128)}, u32[]{:S(2)}) copy-start(f32[2,512]{1,0:T(2,128)} %param.19) | copy-start | bytes 12292
  0.7 15.5 %copy-start.19 = (bf16[2,512,8]{1,2,0:T(8,128)(2,1)S(1)}, bf16[2,512,8]{1,2,0:T(8,128)(2,1)}, u32[]{:S(2)}) copy-start(bf16[2,512,8]{1,2,0:T(8,128)(2,1)} %param.22) | copy-start | bytes 49156
  0.7 15.5 %copy-start.16 = (bf16[2,512,256]{2,1,0:T(8,128)(2,1)S(1)}, bf16[2,512,256]{2,1,0:T(8,128)(2,1)}, u32[]{:S(2)}) copy-start(bf16[2,512,256]{2,1,0:T(8,128)(2,1)} %param.21) | copy-start | bytes 1572868
  2.3 18.1 %copy-start.5 = (s32[16]{0:T(128)}, s32[16]{0:T(128)S(1)}, u32[]{:S(2)}) copy-start(s32[16]{0:T(128)S(1)} %select_reduce_fusion.slots) | copy-start | bytes 196
  2.3 18.1 %copy-start.22 = (f32[2,8]{1,0:T(2,128)S(1)}, f32[2,8]{1,0:T(2,128)}, u32[]{:S(2)}) copy-start(f32[2,8]{1,0:T(2,128)} %param.27) | copy-start | bytes 196
  2.3 18.1 %copy-start.23 = (f32[2,8]{1,0:T(2,128)S(1)}, f32[2,8]{1,0:T(2,128)}, u32[]{:S(2)}) copy-start(f32[2,8]{1,0:T(2,128)} %param.26) | copy-start | bytes 196
  2.4 18.1 %copy-start.24 = (f32[2,8]{1,0:T(2,128)S(1)}, f32[2,8]{1,0:T(2,128)}, u32[]{:S(2)}) copy-start(f32[2,8]{1,0:T(2,128)} %param.25) | copy-start | bytes 196
  2.4 18.7 %copy-start.18 = (bf16[2,8,3,256]{3,1,2,0:T(8,128)(2,1)S(1)}, bf16[2,8,3,256]{3,1,2,0:T(8,128)(2,1)}, u32[]{:S(2)}) copy-start(bf16[2,8,3,256]{3,1,2,0:T(8,128)(2,1)} %param.31) | copy-start | bytes 73732
  2.4 18.7 %copy-start.17 = (bf16[2,8,3,512]{3,1,2,0:T(8,128)(2,1)S(1)}, bf16[2,8,3,512]{3,1,2,0:T(8,128)(2,1)}, u32[]{:S(2)}) copy-start(bf16[2,8,3,512]{3,1,2,0:T(8,128)(2,1)} %param.30) | copy-start | bytes 147460
  6.2 0.8 copy-start.8
  7.0 0.8 copy-start.10
  7.8 0.8 copy-start.12
  8.6 0.8 copy-start.13
  9.3 0.8 copy-start.14
  10.2 25.7 %collective-permute-start = (bf16[2,2,8,64,128]{4,3,2,1,0:T(8,128)(2,1)}, bf16[2,2,8,64,128]{4,3,2,1,0:T(8,128)(2,1)}, u32[]{:S(2)}, u32[]{:S(2)}) collective-permute-start(bf16[2,2,8,64,128]{4,3,2,1,0:T(8,128)(2,1)} %get-tuple-element.51), channel_id=1, source_target_pairs={{0,1},{1,2},{2,3},{3,4},{4,5},{5,6},{6,7},{7,0},{8,9},{9,10},{10,1... | collective-permute-start | bytes 1572872 | tf_op jit(solution)/shard_map/ppermute | solution.py:566
  13.1 24.9 %collective-permute-start.1 = (bf16[2,2,8,64,128]{4,3,2,1,0:T(8,128)(2,1)}, bf16[2,2,8,64,128]{4,3,2,1,0:T(8,128)(2,1)}, u32[]{:S(2)}, u32[]{:S(2)}) collective-permute-start(bf16[2,2,8,64,128]{4,3,2,1,0:T(8,128)(2,1)} %get-tuple-element.52), channel_id=1, source_target_pairs={{0,7},{1,0},{2,1},{3,2},{4,3},{5,4},{6,5},{7,6},{8,15},{9,8},{10,9... | collective-permute-start | bytes 1572872 | tf_op jit(solution)/shard_map/ppermute | solution.py:566
  25.4 2.4 %copy-start.15 = (bf16[512,120]{1,0:T(8,128)(2,1)}, bf16[512,120]{1,0:T(8,128)(2,1)S(1)}, u32[]{:S(2)}) copy-start(bf16[512,120]{1,0:T(8,128)(2,1)S(1)} %broadcast.25) | copy-start | bytes 368644
  27.7 42.1 %copy-start.2 = (f32[2,4,512]{2,1,0:T(4,128)S(1)}, f32[2,4,512]{2,1,0:T(4,128)}, u32[]{:S(2)}) copy-start(f32[2,4,512]{2,1,0:T(4,128)} %inner_kernel.3) | copy-start | bytes 49156
  27.8 42.1 %copy-start.3 = (f32[2,4,256]{2,1,0:T(4,128)S(1)}, f32[2,4,256]{2,1,0:T(4,128)}, u32[]{:S(2)}) copy-start(f32[2,4,256]{2,1,0:T(4,128)} %proj_kernel.3) | copy-start | bytes 24580
  27.8 42.1 %copy-start.4 = (s32[8]{0:T(128)S(1)}, s32[8]{0:T(128)}, u32[]{:S(2)}) copy-start(s32[8]{0:T(128)} %accepted.3) | copy-start | bytes 100
  30.3 39.6 %copy-start = (f32[2,8,8,64,128]{4,3,2,1,0:T(8,128)S(1)}, f32[2,8,8,64,128]{4,3,2,1,0:T(8,128)}, u32[]{:S(2)}) copy-start(f32[2,8,8,64,128]{4,3,2,1,0:T(8,128)} %state_ref.5) | copy-start | bytes 12582916
  38.0 0.8 copy-start.1
  60.9 154.1 %collective-permute-start.2 = (bf16[2,2,8,64,128]{4,3,2,1,0:T(8,128)(2,1)}, bf16[2,2,8,64,128]{4,3,2,1,0:T(8,128)(2,1)S(1)}, u32[]{:S(2)}, u32[]{:S(2)}) collective-permute-start(bf16[2,2,8,64,128]{4,3,2,1,0:T(8,128)(2,1)} %copy-done.14), channel_id=1, source_target_pairs={{0,2},{1,3},{2,4},{3,5},{4,6},{5,7},{6,0},{7,1},{8,10},{9,11},{10,... | collective-permute-start | bytes 1572872 | tf_op jit(solution)/shard_map/ppermute | solution.py:566
  64.4 150.7 %collective-permute-start.4 = (bf16[2,2,8,64,128]{4,3,2,1,0:T(8,128)(2,1)}, bf16[2,2,8,64,128]{4,3,2,1,0:T(8,128)(2,1)S(1)}, u32[]{:S(2)}, u32[]{:S(2)}) collective-permute-start(bf16[2,2,8,64,128]{4,3,2,1,0:T(8,128)(2,1)} %copy-done.13), channel_id=1, source_target_pairs={{0,4},{1,5},{2,6},{3,7},{4,0},{5,1},{6,2},{7,3},{8,12},{9,13},{10,... | collective-permute-start | bytes 1572872 | tf_op jit(solution)/shard_map/ppermute | solution.py:566
  69.9 145.2 %collective-permute-start.6 = (bf16[2,2,8,64,128]{4,3,2,1,0:T(8,128)(2,1)}, bf16[2,2,8,64,128]{4,3,2,1,0:T(8,128)(2,1)S(1)}, u32[]{:S(2)}, u32[]{:S(2)}) collective-permute-start(bf16[2,2,8,64,128]{4,3,2,1,0:T(8,128)(2,1)} %copy-done.12), channel_id=1, source_target_pairs={{0,6},{1,7},{2,0},{3,1},{4,2},{5,3},{6,4},{7,5},{8,14},{9,15},{10,... | collective-permute-start | bytes 1572872 | tf_op jit(solution)/shard_map/ppermute | solution.py:566
  69.9 0.7 copy-start.7
  70.6 87.3 %copy-start.11 = (bf16[2,2,8,64,128]{4,3,2,1,0:T(8,128)(2,1)S(1)}, bf16[2,2,8,64,128]{4,3,2,1,0:T(8,128)(2,1)}, u32[]{:S(2)}) copy-start(bf16[2,2,8,64,128]{4,3,2,1,0:T(8,128)(2,1)} %copy-done.10) | copy-start | bytes 1572868
  70.6 93.1 %copy-start.9 = (bf16[2,2,8,64,128]{4,3,2,1,0:T(8,128)(2,1)S(1)}, bf16[2,2,8,64,128]{4,3,2,1,0:T(8,128)(2,1)}, u32[]{:S(2)}) copy-start(bf16[2,2,8,64,128]{4,3,2,1,0:T(8,128)(2,1)} %copy-done.8) | copy-start | bytes 1572868
  157.9 57.1 %collective-permute-start.3 = (bf16[2,2,8,64,128]{4,3,2,1,0:T(8,128)(2,1)S(1)}, bf16[2,2,8,64,128]{4,3,2,1,0:T(8,128)(2,1)S(1)}, u32[]{:S(2)}, u32[]{:S(2)}) collective-permute-start(bf16[2,2,8,64,128]{4,3,2,1,0:T(8,128)(2,1)S(1)} %copy-done.11), channel_id=1, source_target_pairs={{0,3},{1,4},{2,5},{3,6},{4,7},{5,0},{6,1},{7,2},{8,11},{9,12},{10,... | collective-permute-start | bytes 1572872 | tf_op jit(solution)/shard_map/ppermute | solution.py:566
  163.7 51.4 %collective-permute-start.5 = (bf16[2,2,8,64,128]{4,3,2,1,0:T(8,128)(2,1)S(1)}, bf16[2,2,8,64,128]{4,3,2,1,0:T(8,128)(2,1)S(1)}, u32[]{:S(2)}, u32[]{:S(2)}) collective-permute-start(bf16[2,2,8,64,128]{4,3,2,1,0:T(8,128)(2,1)S(1)} %copy-done.9), channel_id=1, source_target_pairs={{0,5},{1,6},{2,7},{3,0},{4,1},{5,2},{6,3},{7,4},{8,13},{9,14},{10,... | collective-permute-start | bytes 1572872 | tf_op jit(solution)/shard_map/ppermute | solution.py:566
  163.7 51.4 %copy-start.6 = (s32[16]{0:T(128)S(1)}, s32[16]{0:T(128)}, u32[]{:S(2)}) copy-start(s32[16]{0:T(128)} %copy-done.5) | copy-start | bytes 196
